TPU v7x, 256 devices: a whole 4x4x8 slice. The times are simulated.
256 devices in a mesh: rep: 16 (over y, x), tp: 16 (over z, core).
Axes of the slice: x: 4, y: 4, z: 8, core: 2. Of those that a mesh axis runs over, the one named last changes fastest.
Arguments:
- inputs: bfloat16 [2, 8192, 8192], P(None, 'rep', 'tp'), may hold values from -6 to 6
- targets: bfloat16 [2, 8192, 2048], P(None, 'rep', 'tp'), may hold values from -6 to 6
- weight: bfloat16 [8192, 2048], P('tp'), may hold values from -0.0625 to 0.0625
- momentum: float32 [16, 8192, 2048], P('rep', 'tp'), may hold values from -0.8 to 0.8
- indices: int32 [2, 16, 64, 16, 2], P(None, None, 'tp'), may hold values from 0 to 127, as said below
Outputs:
- new_weight: bfloat16 [8192, 2048], P('tp')
- new_momentum: float32 [16, 8192, 2048], P('rep', 'tp')
Inputs may be any that keep to these rules, and one draw needn't show every extreme that they name: `indices`: the 2 entries of each block's list are distinct rows of the block's transform.
All inputs are finite; a program needn't handle non-finite values.
Results may differ from a plain program's by a relative error of at most 0.0085.
Values may be sent and summed in bfloat16 or wider, within the bound.
A program may use at most 128 MiB of HBM per device.

v0:
```python
import jax
import jax.numpy as jnp
from jax import lax
from jax.sharding import PartitionSpec as P

BLOCK = 128
STEPS = 2
TOK_DEV = 512


def dct_table(size):
    rows = jnp.arange(size, dtype=jnp.float32)[:, None]
    cols = jnp.arange(size, dtype=jnp.float32)[None, :]
    scale = jnp.where(rows == 0, jnp.sqrt(1.0 / size), jnp.sqrt(2.0 / size))
    return scale * jnp.cos(jnp.pi * (2.0 * cols + 1.0) * rows / (2.0 * size))


def local(inputs, targets, weight, momentum, indices):
    high = lax.Precision.HIGHEST
    basis = dct_table(BLOCK)
    rows_local = weight.shape[0]
    cols_all = weight.shape[1]
    nbr = rows_local // BLOCK
    nbc = cols_all // BLOCK
    moment = momentum[0]
    weight_now = weight
    replica = lax.axis_index("rep")
    for step in range(STEPS):
        acts = inputs[step]
        partial_value = jnp.dot(acts, weight_now, preferred_element_type=jnp.float32)
        out_cols = lax.psum_scatter(partial_value, "tp", scatter_dimension=1, tiled=True)
        errors = (out_cols - targets[step].astype(jnp.float32)).astype(jnp.bfloat16)
        grad = (
            lax.dot_general(
                acts,
                lax.all_gather(errors, "tp", axis=1, tiled=True),
                (((0,), (0,)), ((), ())),
                preferred_element_type=jnp.float32,
            )
            / TOK_DEV
        )
        updated = 0.9 * moment + grad
        blocks = updated.reshape(nbr, BLOCK, nbc, BLOCK)
        every_pick = (indices[step][..., None] == jnp.arange(BLOCK, dtype=jnp.int32)).astype(
            jnp.float32
        )
        own_pick = lax.dynamic_index_in_dim(every_pick, replica, 0, keepdims=False)
        rows_sel = jnp.einsum("abjk,kn->abjn", own_pick, basis, precision=high)
        inner = jnp.einsum("abjn,anbm->abjm", rows_sel, blocks, precision=high)
        coeffs = jnp.einsum("abjm,cm->abjc", inner, basis, precision=high)
        back = jnp.einsum("abjc,cm->abjm", coeffs, basis, precision=high)
        decoded = jnp.einsum("abjn,abjm->anbm", rows_sel, back, precision=high).reshape(
            rows_local, cols_all
        )
        moment = updated - decoded
        update = lax.psum(decoded, "rep")
        weight_now = (weight_now.astype(jnp.float32) - 0.1 * update).astype(jnp.bfloat16)
    return (weight_now, moment[None])


def solution(mesh):
    in_specs = (
        P(None, "rep", "tp"),
        P(None, "rep", "tp"),
        P("tp", None),
        P("rep", "tp", None),
        P(None, None, "tp", None, None),
    )
    out_specs = (P("tp", None), P("rep", "tp", None))
    return jax.shard_map(local, mesh=mesh, in_specs=in_specs, out_specs=out_specs, check_vma=False)
```

profile of v0, /device:TPU:1, one launch (start us, length us, event | category | flops | bytes accessed | tf_op | source)
XLA Modules:
  0.0 542.5 jit_solution(13660206204499909125)
XLA Ops:
  7.2 0.0 reduce-scatter.3.cloned.1.call-start
  7.2 5.1 fusion.7
  12.3 0.0 reduce-scatter.3.cloned.1.call-update
  12.3 0.0 all-gather.3.cloned.1.call-start
  12.4 63.4 %reduce-scatter.3.cloned.1.call-done = f32[512,128]{1,0:T(8,128)} async-done(((f32[512,2048]{1,0:T(8,128)}), f32[512,128]{1,0:T(8,128)}) %reduce-scatter.3.cloned.1.call-update) | async-done | bytes 262160 | tf_op jit(solution)/shard_map/reduce_scatter | solution.py:31
  75.8 1.6 fusion.14
  77.4 0.0 all-gather.3.cloned.1.call-update
  77.5 0.0 all-reduce.3.cloned.1.call-start
  77.5 5.4 %copy.8 = f32[1,512,2048]{1,2,0:T(8,128)} copy(f32[1,512,2048]{2,1,0:T(8,128)} %param.8) | data formatting | bytes 8388608 | tf_op args[3]
  83.0 0.4 fusion.25
  83.5 37.8 %all-gather.3.cloned.1.call-done = bf16[512,2048]{1,0:T(8,128)(2,1)} async-done(((bf16[512,128]{1,0:T(8,128)(2,1)}), bf16[512,2048]{1,0:T(8,128)(2,1)}) %all-gather.3.cloned.1.call-update) | async-done | bytes 2097168 | tf_op jit(solution)/shard_map/all_gather | solution.py:36
  121.3 6.3 %bitcast_add_fusion.1 = f32[512,2048]{0,1:T(8,128)} fusion(f32[1,512,2048]{1,2,0:T(8,128)} %copy.8, bf16[512,2048]{1,0:T(8,128)(2,1)} %all-gather.3.cloned.1.call-done, bf16[2,512,512]{2,1,0:T(8,128)(2,1)S(1)} %copy-done.2), kind=kOutput, calls=%fused_computation.3 | convolution fusion | flops 1076887552 | bytes 11010048 | tf_op jit(solution)/shard_map/dot_general | solution.py:34
  127.5 5.2 reshape.40
  132.8 8.5 %fusion.2 = f32[4,16,2,128]{3,2,1,0:T(2,128)S(1)} fusion(f32[4,128,16,128]{1,0,3,2:T(4,128)} %reshape.40, f32[4,16,2,128]{3,1,2,0:T(8,128)S(1)} %fusion.25), kind=kOutput, calls=%fused_computation.6 | convolution fusion | flops 25165824 | bytes 4325376 | tf_op jit(solution)/shard_map/abjn,anbm->abjm/dot_general | solution.py:49
  141.3 0.5 fusion.23
  141.8 0.5 fusion.21
  142.3 6.7 %convolution_bitcast_fusion.2 = f32[4,128,16,128]{1,3,2,0:T(8,128)S(1)} fusion(f32[4,16,2,128]{3,1,2,0:T(8,128)S(1)} %fusion.21, f32[4,16,2,128]{3,1,2,0:T(8,128)S(1)} %fusion.25), kind=kOutput, calls=%fused_computation.13 | convolution fusion | flops 25165824 | bytes 4325376 | tf_op jit(solution)/shard_map/abjn,abjm->anbm/dot_general | solution.py:52
  149.0 2.8 copy.10
  151.8 2.7 copy.55
  154.5 0.5 copy-done.1
  155.0 0.0 all-reduce.3.cloned.1.call-update
  155.1 0.0 reduce-scatter.5.cloned.1.call-start
  155.1 3.1 copy.7
  158.2 109.2 %all-reduce.3.cloned.1.call-done = f32[512,2048]{0,1:T(8,128)} async-done(((f32[512,2048]{0,1:T(8,128)}), f32[512,2048]{0,1:T(8,128)}) %all-reduce.3.cloned.1.call-update) | async-done | bytes 4194320 | tf_op jit(solution)/shard_map/psum | solution.py:56
  267.4 5.5 %convolution_bitcast_fusion = f32[512,2048]{1,0:T(8,128)} fusion(bf16[2,512,512]{2,1,0:T(8,128)(2,1)S(1)} %copy-done.2, f32[512,2048]{0,1:T(8,128)} %all-reduce.3.cloned.1.call-done, bf16[512,2048]{0,1:T(8,128)(2,1)S(1)} %copy.7), kind=kOutput, calls=%fused_computation.11 | convolution fusion | flops 1077936128 | bytes 11010048 | tf_op jit(solution)/shard_map/dot_general | solution.py:30
  272.9 0.0 reduce-scatter.5.cloned.1.call-update
  272.9 0.0 all-gather.5.cloned.1.call-start
  273.0 59.8 %reduce-scatter.5.cloned.1.call-done = f32[512,128]{1,0:T(8,128)} async-done(((f32[512,2048]{1,0:T(8,128)}), f32[512,128]{1,0:T(8,128)}) %reduce-scatter.5.cloned.1.call-update) | async-done | bytes 262160 | tf_op jit(solution)/shard_map/reduce_scatter | solution.py:31
  332.8 1.6 fusion.13
  334.4 0.0 all-gather.5.cloned.1.call-update
  334.4 0.0 all-reduce.5.cloned.1.call-start
  334.5 0.4 fusion.19
  334.9 43.0 %all-gather.5.cloned.1.call-done = bf16[512,2048]{1,0:T(8,128)(2,1)} async-done(((bf16[512,128]{1,0:T(8,128)(2,1)}), bf16[512,2048]{1,0:T(8,128)(2,1)}) %all-gather.5.cloned.1.call-update) | async-done | bytes 2097168 | tf_op jit(solution)/shard_map/all_gather | solution.py:36
  377.9 7.7 %bitcast_add_fusion = f32[512,2048]{0,1:T(8,128)} fusion(f32[512,2048]{0,1:T(8,128)} %bitcast_add_fusion.1, bf16[512,2048]{1,0:T(8,128)(2,1)} %all-gather.5.cloned.1.call-done, bf16[2,512,512]{2,1,0:T(8,128)(2,1)S(1)} %copy-done.2, f32[256,8,4,128]{3,2,1,0:T(4,128)} %bitcast.85), kind=kOutput, calls=%fused_computation.2 | convolution fusion | flops 1077936128 | bytes 15204352 | tf_op jit(solution)/shard_map/dot_general | solution.py:34
  385.6 5.3 reshape.42
  390.9 8.3 %fusion = f32[4,16,2,128]{3,2,1,0:T(2,128)S(1)} fusion(f32[4,128,16,128]{1,0,3,2:T(4,128)} %reshape.42, f32[4,16,2,128]{3,1,2,0:T(8,128)S(1)} %fusion.19), kind=kOutput, calls=%fused_computation.4 | convolution fusion | flops 25165824 | bytes 4325376 | tf_op jit(solution)/shard_map/abjn,anbm->abjm/dot_general | solution.py:49
  399.3 0.5 fusion.17
  399.8 0.5 fusion.15
  400.2 6.7 %convolution_bitcast_fusion.1 = f32[4,128,16,128]{1,3,2,0:T(8,128)S(1)} fusion(f32[4,16,2,128]{3,1,2,0:T(8,128)S(1)} %fusion.15, f32[4,16,2,128]{3,1,2,0:T(8,128)S(1)} %fusion.19), kind=kOutput, calls=%fused_computation.12 | convolution fusion | flops 25165824 | bytes 4325376 | tf_op jit(solution)/shard_map/abjn,abjm->anbm/dot_general | solution.py:52
  406.9 2.8 copy.12
  409.7 2.7 copy.54
  412.4 0.5 copy-done
  412.9 0.0 all-reduce.5.cloned.1.call-update
  412.9 6.4 %subtract_bitcast_fusion = f32[1,512,2048]{1,2,0:T(8,128)} fusion(f32[512,2048]{0,1:T(8,128)} %bitcast_add_fusion, f32[256,8,4,128]{3,2,1,0:T(4,128)} %bitcast.83), kind=kLoop, calls=%fused_computation.8 | loop fusion | flops 1048576 | bytes 12582912 | tf_op jit(solution)/shard_map/broadcast_in_dim | solution.py:58
  419.4 5.4 copy.14
  424.7 100.6 %all-reduce.5.cloned.1.call-done = f32[512,2048]{0,1:T(8,128)} async-done(((f32[512,2048]{0,1:T(8,128)}), f32[512,2048]{0,1:T(8,128)}) %all-reduce.5.cloned.1.call-update) | async-done | bytes 4194320 | tf_op jit(solution)/shard_map/psum | solution.py:56
  525.3 6.1 %subtract_convert_fusion = bf16[512,2048]{0,1:T(8,128)(2,1)} fusion(f32[512,2048]{0,1:T(8,128)} %all-reduce.5.cloned.1.call-done, f32[512,2048]{0,1:T(8,128)} %all-reduce.3.cloned.1.call-done, bf16[512,2048]{0,1:T(8,128)(2,1)S(1)} %copy.7), kind=kLoop, calls=%fused_computation.9 | loop fusion | flops 8388608 | bytes 12582912 | tf_op jit(solution)/shard_map/convert_element_type | solution.py:57
  531.4 3.9 copy.13
  (11 shorter events, 0.1 us)
Async XLA Ops:
  7.2 68.6 %copy-start.3 = (bf16[2,512,128]{2,1,0:T(8,128)(2,1)S(1)}, bf16[2,512,128]{2,1,0:T(8,128)(2,1)}, u32[]{:S(2)}) copy-start(bf16[2,512,128]{2,1,0:T(8,128)(2,1)} %param.6) | copy-start | bytes 786436
  7.2 68.6 %reduce-scatter.3.cloned.1.call-start = ((), (), s32[]{:S(2)}) async-start(), calls=%async_computation.2 | async-start | bytes 4456448 | tf_op jit(solution)/shard_map/reduce_scatter | solution.py:31
  12.3 109.0 %all-gather.3.cloned.1.call-start = ((), (), s32[]{:S(2)}) async-start(), calls=%async_computation.3 | async-start | bytes 2228224 | tf_op jit(solution)/shard_map/all_gather | solution.py:36
  77.5 190.0 %all-reduce.3.cloned.1.call-start = ((), (), s32[]{:S(2)}) async-start(), calls=%async_computation.4 | async-start | bytes 8388608 | tf_op jit(solution)/shard_map/psum | solution.py:56
  77.5 5.5 %copy-start.4 = (s32[2,16,4,16,2]{3,4,2,1,0:T(2,128)S(1)}, s32[2,16,4,16,2]{3,4,2,1,0:T(2,128)}, u32[]{:S(2)}) copy-start(s32[2,16,4,16,2]{3,4,2,1,0:T(2,128)} %param.9) | copy-start | bytes 49156
  77.5 43.7 %copy-start.2 = (bf16[2,512,512]{2,1,0:T(8,128)(2,1)S(1)}, bf16[2,512,512]{2,1,0:T(8,128)(2,1)}, u32[]{:S(2)}) copy-start(bf16[2,512,512]{2,1,0:T(8,128)(2,1)} %param.5) | copy-start | bytes 3145732
  151.8 3.3 copy-start.1
  155.1 177.7 %reduce-scatter.5.cloned.1.call-start = ((), (), s32[]{:S(2)}) async-start(), calls=%async_computation.5 | async-start | bytes 4456448 | tf_op jit(solution)/shard_map/reduce_scatter | solution.py:31
  272.9 105.0 %all-gather.5.cloned.1.call-start = ((), (), s32[]{:S(2)}) async-start(), calls=%async_computation.6 | async-start | bytes 2228224 | tf_op jit(solution)/shard_map/all_gather | solution.py:36
  334.4 190.9 %all-reduce.5.cloned.1.call-start = ((), (), s32[]{:S(2)}) async-start(), calls=%async_computation.7 | async-start | bytes 8388608 | tf_op jit(solution)/shard_map/psum | solution.py:56
  409.7 3.2 copy-start
Sparse Core Ops, SparseCore 0:
  12.4 63.3 reduce-scatter.2
  78.1 43.0 all-gather.2
  155.2 112.2 all-reduce.2
  273.0 59.7 reduce-scatter.4
  335.0 42.8 all-gather.4
  413.0 112.2 all-reduce.4
where the time goes:
time: 548 us; the launch traced here: 543 us
  waiting for transfers between devices  414 us (76%)
  matrix products  57.5 us (10%)
  local copies, waits for them, and re-layouts  40.4 us (7%)
  other arithmetic  15.8 us (3%)
  between operations  14.6 us (3%)
    psum x2, waiting for transfers between devices, local(): update = lax.psum(decoded, 'rep')  210 us
    reduce_scatter x2, waiting for transfers between devices, local(): lax.psum_scatter(partial_value, 'tp', scatter_dimension=1, tiled=True)  123 us
    all_gather x2, waiting for transfers between devices, local(): lax.all_gather(errors, 'tp', axis=1, tiled=True)  80.8 us
    unnamed x16, local copies, waits for them, and re-layouts  24.3 us
    dot_general x2, matrix products, local(): inner = jnp.einsum('abjn,anbm->abjm', rows_sel, blocks, precision=high)  16.9 us
    dot_general x2, matrix products, local(): lax.dot_general(acts, lax.all_gather(errors, 'tp', axis=1, tiled=True), (...  14 us
    dot_general x2, matrix products, local(): jnp.einsum('abjn,abjm->anbm', rows_sel, back, precision=high)  13.4 us
  transfers between devices with their start and end apart: 6, of which 6 were waited for; matrix products, arithmetic and copies ran while one was open for 4% of the time, Pallas kernels for 0%

commit v1 on v0

v1 whole, which is shorter than its diff:
```python
import functools

import jax
import jax.numpy as jnp
import ml_dtypes
import numpy as np
from jax import lax
from jax.experimental import pallas as pl
from jax.experimental.pallas import tpu as pltpu
from jax.sharding import PartitionSpec as P

MESH = pl.DeviceIdType.MESH
BLOCK = 128
STEPS = 2
TOK = 512
NZ = 8
ROWS = 512
NSUB = 4
SUB = TOK // NSUB
F32 = jnp.float32
BF16 = jnp.bfloat16


def basis_parts():
    k = np.arange(BLOCK, dtype=np.float64)[:, None]
    n = np.arange(BLOCK, dtype=np.float64)[None, :]
    scale = np.where(k == 0, np.sqrt(1.0 / BLOCK), np.sqrt(2.0 / BLOCK))
    table = (scale * np.cos(np.pi * (2.0 * n + 1.0) * k / (2.0 * BLOCK))).T
    high = table.astype(ml_dtypes.bfloat16)
    low = (table - high.astype(np.float64)).astype(ml_dtypes.bfloat16)
    return np.stack([high, low])


def iota(shape, axis):
    return lax.broadcasted_iota(jnp.int32, shape, axis)


def kernel(
    n_rep,
    x_ref, t_ref, w_ref, m_ref, idx_ref, bt_ref,
    w_out, m_out,
    xa, xt, tv, wb, mb, ix, ixp, bt, ic, comb, rtf, lu, rtb,
    yp, ys, rl, ef, lx, xr_send, xr_land, rm_send, rm_land, s_send, sn, sall,
    load_sem, pair_send, pair_recv, rs_send, rs_recv, ag_send, ag_recv,
    xr_ssem, xr_rsem, rm_ssem, rm_rsem, sa_ssem, sa_rsem, sp_ssem, sp_rsem,
    pl_ssem, pl_rsem, fw_ssem, fw_rsem, out_sem, outp_ssem, outp_rsem,
):
    r = lax.axis_index("rep")
    me = lax.axis_index("tp")
    z = me // 2
    c = me % 2
    o = 1 - c
    lanes = n_rep * 16
    d = 1 - 2 * c
    partner = {"tp": 2 * z + o}

    def zz(k):
        return lax.rem(z + k + 2 * NZ, NZ)

    long_to = {"tp": 2 * zz(d) + c}
    short_to = {"tp": 2 * zz(-d) + c}

    def remote(src, dst, s, v, dev):
        return pltpu.make_async_remote_copy(
            src_ref=src, dst_ref=dst, send_sem=s, recv_sem=v, device_id=dev, device_id_type=MESH
        )

    def cols(j, h):
        return pl.ds(pl.multiple_of((2 * j + h) * BLOCK, BLOCK), BLOCK)

    half_own = pl.ds(pl.multiple_of(c * ROWS, ROWS), ROWS)
    half_other = pl.ds(pl.multiple_of(o * ROWS, ROWS), ROWS)

    loads = {}

    def load(name, k, src, dst):
        copy = pltpu.make_async_copy(src, dst, load_sem.at[k])
        copy.start()
        loads[name] = copy

    load("x0", 0, x_ref.at[0], xa.at[0, c])
    for j in range(NZ):
        load(("w", j), 8 + j, w_ref.at[:, cols(j, c)], wb.at[j, half_own])
    load("bt", 1, bt_ref, bt)
    load("ix", 2, idx_ref, ix)
    load("x1", 3, x_ref.at[1], xa.at[1, c])
    load("t", 4, t_ref, tv)
    for j in range(NZ):
        load(("m", j), 16 + j, m_ref.at[0, :, pl.ds(2 * BLOCK * j, 2 * BLOCK)], mb.at[j])

    barrier = pltpu.get_barrier_semaphore()
    for k in range(1, 2 * NZ):
        pl.semaphore_signal(barrier, inc=1, device_id={"tp": lax.rem(me + k, 2 * NZ)}, device_id_type=MESH)
    for k in range(1, n_rep):
        pl.semaphore_signal(barrier, inc=1, device_id={"rep": lax.rem(r + k, n_rep)}, device_id_type=MESH)
    pl.semaphore_wait(barrier, 2 * NZ - 1 + n_rep - 1)

    pairs = []

    def pair(k, src, dst):
        copy = remote(src, dst, pair_send.at[k], pair_recv.at[k], partner)
        copy.start()
        pairs.append(copy)

    pair(0, x_ref.at[0], xa.at[0, c])
    for j in range(NZ):
        pair(1 + j, w_ref.at[:, cols(j, o)], wb.at[j, half_own])
    pair(9, idx_ref.at[:, o], ixp)
    pair(10, x_ref.at[1], xa.at[1, c])

    order = [(zz(4 * d), zz(-3 * d)), (zz(3 * d), zz(-2 * d)), (zz(2 * d), zz(-d)), (zz(d), z)]

    def forward(s, k):
        p, q = order[k]
        for i in range(2):
            rows = pl.ds(i * 256, 256)
            acc = jnp.zeros((256, 2 * BLOCK), F32)
            for h in range(2):
                w = jnp.concatenate([wb[p, h * ROWS:(h + 1) * ROWS], wb[q, h * ROWS:(h + 1) * ROWS]], axis=1)
                acc += jnp.dot(xa[s, h, rows], w, preferred_element_type=F32)
            yp[2 * k, rows] = acc[:, :BLOCK]
            yp[2 * k + 1, rows] = acc[:, BLOCK:]
            if k == 0:
                ys[s, 0, rows] = acc[:, :BLOCK].astype(BF16)
                ys[s, 1, rows] = acc[:, BLOCK:].astype(BF16)

    def rs_copy(s, way, h, u):
        slot = h - 1 if way == 0 else 3 + h
        rows = pl.ds(u * SUB, SUB)
        if h == 1:
            src = ys.at[s, way, rows]
        else:
            src = rl.at[s, slot - 1, rows]
        return remote(src, rl.at[s, slot, rows], rs_send.at[s, slot, u], rs_recv.at[s, slot, u], (long_to, short_to)[way])

    def rs_first(s):
        for u in range(NSUB):
            for way in range(2):
                rs_copy(s, way, 1, u).start()

    def rs_hop(s, h):
        for u in range(NSUB):
            rows = pl.ds(u * SUB, SUB)
            for way in range(2):
                if h > 4 - way:
                    continue
                rs_copy(s, way, h - 1, u).wait_recv()
                slot = h - 2 if way == 0 else 2 + h
                rl[s, slot, rows] = (rl[s, slot, rows].astype(F32) + yp[2 * (h - 1) + way, rows]).astype(BF16)
                rs_copy(s, way, h, u).start()

    def rs_last(s):
        for u in range(NSUB):
            rows = pl.ds(u * SUB, SUB)
            rs_copy(s, 1, 3, u).wait_recv()
            rs_copy(s, 0, 4, u).wait_recv()
            total = yp[7, rows] + rl[s, 3, rows].astype(F32) + rl[s, 6, rows].astype(F32)
            ef[s, c, z, rows] = (total - tv[s, rows].astype(F32)).astype(BF16)

    def ag_copy(s, way, h, u):
        slot = h - 1 if way == 0 else 3 + h
        rows = pl.ds(u * SUB, SUB)
        origin = zz(-d * (h - 1)) if way == 0 else zz(d * (h - 1))
        block = ef.at[s, c, origin, rows]
        return remote(block, block, ag_send.at[s, slot, u], ag_recv.at[s, slot, u], (long_to, short_to)[way])

    def fw_copy(s, k):
        origin = zz(-d * k) if k < 5 else zz(d * (k - 4))
        block = ef.at[s, c, origin]
        return remote(block, block, fw_ssem.at[s, k], fw_rsem.at[s, k], partner)

    def ag_hop(s, h):
        for u in range(NSUB):
            for way in range(2):
                if h > 1 and h <= 5 - way:
                    ag_copy(s, way, h - 1, u).wait_recv()
                if h <= 4 - way:
                    ag_copy(s, way, h, u).start()
        if h == 1:
            fw_copy(s, 0).start()
        else:
            for way in range(2):
                if h <= 5 - way:
                    fw_copy(s, h - 1 if way == 0 else 3 + h).start()

    def build_replicas(s):
        def body(j, _):
            row = ix[s, c, pl.ds(j, 1)] + ixp[s, pl.ds(j, 1)]
            onehot = jnp.where(iota((BLOCK, lanes), 0) == row, 1.0, 0.0).astype(BF16)
            kept = jnp.dot(bt[0], onehot, preferred_element_type=F32)
            rtb[s, j] = kept.astype(BF16)
            for a in range(8):
                mine = (iota((BLOCK, lanes), 1) % 16) // 2 == a
                lu[s, j, a * BLOCK:(a + 1) * BLOCK] = jnp.where(mine, kept, 0.0).astype(BF16)
            return 0

        lax.fori_loop(0, NZ, body, 0)

    def build_rows(s):
        def body(j, _):
            pick = jnp.where(iota((16, lanes), 1) == 16 * r + iota((16, lanes), 0), 1.0, 0.0).astype(BF16)
            kept = lax.dot_general(pick, rtb[s, j], (((1,), (1,)), ((), ())), preferred_element_type=F32)
            for a in range(8):
                lx[j, :, a * BLOCK:(a + 1) * BLOCK] = jnp.where(iota((16, BLOCK), 0) // 2 == a, kept, 0.0).astype(BF16)
            return 0

        lax.fori_loop(0, NZ, body, 0)
        table = lx[...].reshape(NZ * 16, 2 * ROWS)
        out = jnp.zeros((NZ * 16, TOK), F32)
        for h in range(2):
            out += lax.dot_general(
                table[:, h * ROWS:(h + 1) * ROWS], xa[s, h], (((1,), (1,)), ((), ())), preferred_element_type=F32
            )
        xr_send[s] = out.astype(BF16).reshape(NZ, 16, TOK)

    def xr_copy(s, k):
        to = zz(k)
        return remote(
            xr_send.at[s, to], xr_land.at[s, z], xr_ssem.at[s, k], xr_rsem.at[s, k], {"tp": 2 * to + c}
        )

    def build_own(s):
        lane = iota((NZ, BLOCK), 1)
        shift = lax.rem(2 * lanes - 16 * r - 8 * c, lanes)
        first = pltpu.roll(ix[s, 0], shift, 1)[:, :BLOCK]
        second = pltpu.roll(ix[s, 1], shift, 1)[:, :BLOCK]
        ic[s] = jnp.where(
            lane < 8,
            first,
            jnp.where(
                lane < 16,
                pltpu.roll(first, 8, 1),
                jnp.where(lane < 24, pltpu.roll(second, 16, 1), jnp.where(lane < 32, pltpu.roll(second, 24, 1), -1)),
            ),
        )

        def body(j, _):
            row = ic[s, pl.ds(j, 1)]
            lane = iota((BLOCK, BLOCK), 1)
            hit = iota((BLOCK, BLOCK), 0) == row
            even = (lane // 8) % 2 == 0
            high = jnp.where(hit & even, 1.0, 0.0).astype(BF16)
            low = jnp.where(hit & jnp.logical_not(even), 1.0, 0.0).astype(BF16)
            both = jnp.dot(bt[0], high, preferred_element_type=F32) + jnp.dot(bt[1], low, preferred_element_type=F32)
            comb[s, j] = both
            rtf[s, j] = both + pltpu.roll(both, BLOCK - 8, 1)
            return 0

        lax.fori_loop(0, NZ, body, 0)

    def project(s):
        def body(j, _):
            for h in range(2):
                for a in range(4):
                    block = mb[j, a * BLOCK:(a + 1) * BLOCK, h * BLOCK:(h + 1) * BLOCK]
                    for k in range(2):
                        lane = 16 * h + 2 * a + k
                        column = rtf[s, j, :, lane:lane + 1]
                        rm_send[s, j, h, 2 * a + k:2 * a + k + 1] = jnp.sum(block * column, axis=0, keepdims=True)
            return 0

        lax.fori_loop(0, NZ, body, 0)

    def rm_copy(s, k):
        to = lax.rem(me + k, 2 * NZ)
        return remote(
            rm_send.at[s, to // 2, to % 2], rm_land.at[s, me], rm_ssem.at[s, k], rm_rsem.at[s, k], {"tp": to}
        )

    def kept_rows(s):
        for k in range(1, NZ):
            xr_copy(s, k).wait_recv()
        for k in range(1, 2 * NZ):
            rm_copy(s, k).wait_recv()
        xr_land[s, z] = xr_send[s, z]
        rm_land[s, me] = rm_send[s, z, c]
        table = xr_land[s].reshape(NZ * 16, TOK)
        out = jnp.dot(table, ef[s, c, z], preferred_element_type=F32) * (1.0 / TOK)
        out += 0.9 * rm_land[s].reshape(NZ * 16, BLOCK)
        s_send[s] = out.astype(BF16).reshape(NZ, 16, BLOCK)

    def sa_copy(s, k):
        to = zz(k)
        return remote(
            s_send.at[s, to], sn.at[s, c, z], sa_ssem.at[s, k], sa_rsem.at[s, k], {"tp": 2 * to + c}
        )

    def sp_copy(s):
        return remote(sn.at[s, c], sn.at[s, c], sp_ssem.at[s], sp_rsem.at[s], partner)

    def pl_copy(s, k):
        return remote(
            sn.at[s, c], sall.at[s, r], pl_ssem.at[s, k], pl_rsem.at[s, k], {"rep": lax.rem(r + k, n_rep)}
        )

    def share(s):
        for k in range(1, NZ):
            sa_copy(s, k).start()
        sn[s, c, z] = s_send[s, z]

    def spread(s):
        for k in range(1, NZ):
            sa_copy(s, k).wait_recv()
        for k in range(1, n_rep):
            pl_copy(s, k).start()
        sp_copy(s).start()
        sall[s, r] = sn[s, c]

    def collect(s):
        for k in range(1, n_rep):
            pl_copy(s, k).wait_recv()

    def update(s, j):
        stack = sall[s, :, j].reshape(lanes, BLOCK)
        for i in range(4):
            rows = pl.ds(i * 256, 256)
            change = jnp.dot(lu[s, j, rows], stack, preferred_element_type=F32)
            wb[j, rows] = (wb[j, rows].astype(F32) - 0.1 * change).astype(BF16)

    def momentum(s, j):
        e = jnp.concatenate([ef[s, 0, j], ef[s, 1, j]], axis=1)
        parts = []
        for h in range(2):
            both = sn[s, h, j].astype(F32)
            parts.append(jnp.where(c == 0, both[:8], both[8:]))
        zero = jnp.zeros((8, BLOCK), F32)
        top = jnp.concatenate([parts[0], zero], axis=1)
        low = jnp.concatenate([zero, parts[1]], axis=1)
        right = jnp.concatenate([top, top, low, low, jnp.zeros((BLOCK - 32, 2 * BLOCK), F32)], axis=0).astype(BF16)
        lane = iota((BLOCK, BLOCK), 1)
        for a in range(4):
            rows = pl.ds(a * BLOCK, BLOCK)
            grad = jnp.dot(xt[s, rows], e, preferred_element_type=F32)
            left = jnp.where((lane % 8) // 2 == a, comb[s, j], 0.0).astype(BF16)
            taken = jnp.dot(left, right, preferred_element_type=F32)
            mb[j, rows] = 0.9 * mb[j, rows] + grad * (1.0 / TOK) - taken

    def fw_wait(s):
        for k in range(NZ):
            fw_copy(s, k).wait_recv()

    def turn(s):
        xt[s] = xa[s, c].T

    loads["x0"].wait()
    pairs[0].wait_recv()
    for j in range(NZ):
        loads["w", j].wait()
        pairs[1 + j].wait_recv()
    forward(0, 0)
    rs_first(0)
    loads["bt"].wait()
    loads["ix"].wait()
    pairs[9].wait_recv()
    build_replicas(0)
    build_rows(0)
    for k in range(1, NZ):
        xr_copy(0, k).start()
    for k in range(1, 4):
        forward(0, k)
    rs_hop(0, 2)
    build_own(0)
    for j in range(NZ):
        loads["m", j].wait()
    project(0)
    for k in range(1, 2 * NZ):
        rm_copy(0, k).start()
    rs_hop(0, 3)
    loads["x1"].wait()
    pairs[10].wait_recv()
    build_replicas(1)
    build_rows(1)
    rs_hop(0, 4)
    build_own(1)
    turn(0)
    loads["t"].wait()
    rs_last(0)
    kept_rows(0)
    share(0)
    ag_hop(0, 1)
    spread(0)
    ag_hop(0, 2)
    for k in range(1, NZ):
        xr_copy(1, k).start()
    turn(1)
    collect(0)

    for k in range(4):
        update(0, order[k][0])
        update(0, order[k][1])
        forward(1, k)
        if k == 0:
            rs_first(1)
            ag_hop(0, 3)
    ag_hop(0, 4)
    rs_hop(1, 2)
    ag_hop(0, 5)
    fw_wait(0)
    sp_copy(0).wait_recv()
    lax.fori_loop(0, NZ, lambda j, _: (momentum(0, j), 0)[1], 0)
    rs_hop(1, 3)
    project(1)
    for k in range(1, 2 * NZ):
        rm_copy(1, k).start()
    rs_hop(1, 4)
    rs_last(1)
    kept_rows(1)
    share(1)
    ag_hop(1, 1)
    spread(1)
    ag_hop(1, 2)
    ag_hop(1, 3)
    collect(1)
    out_copies = []
    for j in range(NZ):
        update(1, j)
        own = pltpu.make_async_copy(wb.at[j, half_own], w_out.at[:, cols(j, c)], out_sem.at[j])
        own.start()
        other = remote(wb.at[j, half_other], w_out.at[:, cols(j, c)], outp_ssem.at[j], outp_rsem.at[j], partner)
        other.start()
        out_copies += [own, other]
    ag_hop(1, 4)
    ag_hop(1, 5)
    fw_wait(1)
    sp_copy(1).wait_recv()

    def finish(j, _):
        momentum(1, j)
        pltpu.make_async_copy(
            mb.at[j], m_out.at[0, :, pl.ds(pl.multiple_of(2 * BLOCK * j, 2 * BLOCK), 2 * BLOCK)], out_sem.at[NZ + j]
        ).start()
        return 0

    lax.fori_loop(0, NZ, finish, 0)

    for copy in out_copies:
        copy.wait()
    for j in range(NZ):
        pltpu.make_async_copy(mb.at[j], m_out.at[0, :, pl.ds(2 * BLOCK * j, 2 * BLOCK)], out_sem.at[NZ + j]).wait()
    for copy in pairs:
        copy.wait_send()
    for s in range(STEPS):
        for way in range(2):
            for h in range(1, 5 - way):
                for u in range(NSUB):
                    rs_copy(s, way, h, u).wait_send()
                    ag_copy(s, way, h, u).wait_send()
        for k in range(NZ):
            fw_copy(s, k).wait_send()
        for k in range(1, NZ):
            xr_copy(s, k).wait_send()
            sa_copy(s, k).wait_send()
        for k in range(1, 2 * NZ):
            rm_copy(s, k).wait_send()
        for k in range(1, n_rep):
            pl_copy(s, k).wait_send()
        sp_copy(s).wait_send()


def local(n_rep, inputs, targets, weight, momentum, indices):
    core = lax.axis_index("tp") % 2
    lanes = n_rep * 16
    own = indices.reshape(STEPS, n_rep, 4, NZ, 2, 2).transpose(0, 4, 3, 1, 2, 5)[:, :, :, :, None]
    place = jnp.arange(2, dtype=jnp.int32)[:, None, None] == core
    arranged = jnp.where(place, own, 0).reshape(STEPS, 2, NZ, lanes)
    any_space = pl.BlockSpec(memory_space=pl.ANY)
    dma = pltpu.SemaphoreType.DMA
    scratch = [
        pltpu.VMEM((STEPS, 2, TOK, ROWS), BF16),
        pltpu.VMEM((STEPS, ROWS, TOK), BF16),
        pltpu.VMEM((STEPS, TOK, BLOCK), BF16),
        pltpu.VMEM((NZ, 2 * ROWS, BLOCK), BF16),
        pltpu.VMEM((NZ, ROWS, 2 * BLOCK), F32),
        pltpu.VMEM((STEPS, 2, NZ, lanes), jnp.int32),
        pltpu.VMEM((STEPS, NZ, lanes), jnp.int32),
        pltpu.VMEM((2, BLOCK, BLOCK), BF16),
        pltpu.VMEM((STEPS, NZ, BLOCK), jnp.int32),
        pltpu.VMEM((STEPS, NZ, BLOCK, BLOCK), F32),
        pltpu.VMEM((STEPS, NZ, BLOCK, BLOCK), F32),
        pltpu.VMEM((STEPS, NZ, 2 * ROWS, lanes), BF16),
        pltpu.VMEM((STEPS, NZ, BLOCK, lanes), BF16),
        pltpu.VMEM((NZ, TOK, BLOCK), F32),
        pltpu.VMEM((STEPS, 2, TOK, BLOCK), BF16),
        pltpu.VMEM((STEPS, 7, TOK, BLOCK), BF16),
        pltpu.VMEM((STEPS, 2, NZ, TOK, BLOCK), BF16),
        pltpu.VMEM((NZ, 16, 2 * ROWS), BF16),
        pltpu.VMEM((STEPS, NZ, 16, TOK), BF16),
        pltpu.VMEM((STEPS, NZ, 16, TOK), BF16),
        pltpu.VMEM((STEPS, NZ, 2, 8, BLOCK), F32),
        pltpu.VMEM((STEPS, 2 * NZ, 8, BLOCK), F32),
        pltpu.VMEM((STEPS, NZ, 16, BLOCK), BF16),
        pltpu.VMEM((STEPS, 2, NZ, 16, BLOCK), BF16),
        pltpu.VMEM((STEPS, n_rep, NZ, 16, BLOCK), BF16),
        dma((24,)), dma((11,)), dma((11,)),
        dma((STEPS, 7, NSUB)), dma((STEPS, 7, NSUB)), dma((STEPS, 7, NSUB)), dma((STEPS, 7, NSUB)),
        dma((STEPS, NZ)), dma((STEPS, NZ)), dma((STEPS, 2 * NZ)), dma((STEPS, 2 * NZ)),
        dma((STEPS, NZ)), dma((STEPS, NZ)), dma((STEPS,)), dma((STEPS,)),
        dma((STEPS, n_rep)), dma((STEPS, n_rep)), dma((STEPS, NZ)), dma((STEPS, NZ)),
        dma((2 * NZ,)), dma((NZ,)), dma((NZ,)),
    ]
    return pl.pallas_call(
        functools.partial(kernel, n_rep),
        out_shape=(
            jax.ShapeDtypeStruct(weight.shape, BF16),
            jax.ShapeDtypeStruct(momentum.shape, F32),
        ),
        in_specs=[any_space] * 6,
        out_specs=(any_space, any_space),
        scratch_shapes=scratch,
        compiler_params=pltpu.CompilerParams(
            collective_id=0, has_side_effects=True, vmem_limit_bytes=56 << 20
        ),
    )(inputs, targets, weight, momentum, arranged, jnp.asarray(basis_parts()))


def solution(mesh):
    in_specs = (
        P(None, "rep", "tp"),
        P(None, "rep", "tp"),
        P("tp", None),
        P("rep", "tp", None),
        P(None, None, "tp", None, None),
    )
    out_specs = (P("tp", None), P("rep", "tp", None))
    return jax.shard_map(
        functools.partial(local, mesh.shape["rep"]), mesh=mesh, in_specs=in_specs, out_specs=out_specs, check_vma=False
    )
```

time: 548 us -> 108 us (0.20); the launches traced: 543 us -> 108 us
  waiting for transfers between devices: 414 us -> 0 us
  Pallas kernels: 0 us -> 99.8 us
  matrix products: 57.5 us -> 0 us
  local copies, waits for them, and re-layouts: 40.4 us -> 7.07 us
  other arithmetic: 15.8 us -> 0.64 us
  between operations: 14.6 us -> 0.69 us
    psum x2 -> x0, waiting for transfers between devices: 210 us -> none  [local(): update = lax.psum(decoded, 'rep')]
    reduce_scatter x2 -> x0, waiting for transfers between devices: 123 us -> none  [local(): lax.psum_scatter(partial_value, 'tp', scatter_dimension=1, tiled=True)]
    pallas_call x0 -> x1, Pallas kernels: none -> 99.8 us  [local(): pl.pallas_call(functools.partial(kernel, n_rep), out_shape=(jax.ShapeDtyp...]
    all_gather x2 -> x0, waiting for transfers between devices: 80.8 us -> none  [local(): lax.all_gather(errors, 'tp', axis=1, tiled=True)]
    dot_general x14 -> x0, matrix products: 57.5 us -> none  [the longest x2 16.9 us: local(): inner = jnp.einsum('abjn,anbm->abjm', rows_sel, blocks, precision=high)]
    unnamed x16 -> x5, local copies, waits for them, and re-layouts: 24.3 us -> 6.33 us
    reshape x2 -> x0, local copies, waits for them, and re-layouts: 10.5 us -> none  [local(): blocks = updated.reshape(nbr, BLOCK, nbc, BLOCK)]
    convert_element_type x3 -> x0, other arithmetic: 9.36 us -> none  [the longest x1 6.1 us: local(): (weight_now.astype(jnp.float32) - 0.1 * update).astype(jnp.bfloat16)]
  transfers between devices with their start and end apart: 6 -> 0, of which waited for: 6 -> 0; matrix products, arithmetic and copies ran while one was open for 4% -> 0% of each run, Pallas kernels for 0% -> 0%
where the time goes in v1:
time: 108 us
  Pallas kernels  99.8 us (92%)
  local copies, waits for them, and re-layouts  7.07 us (7%)
    pallas_call x1, Pallas kernels, local(): pl.pallas_call(functools.partial(kernel, n_rep), out_shape=(jax.ShapeDtyp...  99.8 us
    unnamed x5, local copies, waits for them, and re-layouts  6.33 us

profile of v1, /device:TPU:1, one launch (start us, length us, event | category | flops | bytes accessed | tf_op | source)
XLA Modules:
  0.0 108.2 jit_solution(7225166384174582193)
XLA Ops:
  0.7 0.1 broadcast_in_dim.28
  0.7 0.1 broadcast_in_dim.29
  0.9 1.0 copy.9
  1.9 0.2 copy.10
  2.1 0.1 broadcast_in_dim.31
  2.3 0.2 copy.11
  2.4 0.6 broadcast_select_fusion.idx_ref
  3.1 99.8 %shard_map.77 = (bf16[512,2048]{1,0:T(8,128)(2,1)}, f32[1,512,2048]{2,1,0:T(8,128)}) custom-call(bf16[2,512,512]{2,1,0:T(8,128)(2,1)} %x_ref.1, bf16[2,512,128]{2,1,0:T(8,128)(2,1)} %t_ref.1, bf16[512,2048]{1,0:T(8,128)(2,1)} %w_ref.1, f32[1,512,2048]{2,1,0:T(8,128)} %m_ref.1, s32[2,2,8,256]{3,2,1,0:T(8,128)} %broadcast_select_fusion.idx_ref, ...), custom_call_target="tpu_custom_call" | custom-call | tf_op jit(solution)/shard_map/pallas_call | solution.py:501
  102.9 0.0 copy-start
  102.9 3.3 %copy.14 = bf16[512,2048]{1,0:T(8,128)(2,1)} copy(bf16[512,2048]{1,0:T(8,128)(2,1)} %get-tuple-element.4) | data formatting | bytes 4194304
  106.2 0.0 copy-done
  106.2 2.0 %copy.15 = f32[1,512,2048]{2,1,0:T(8,128)} copy(f32[1,512,2048]{2,1,0:T(8,128)S(1)} %copy-done) | data formatting | bytes 8388608
  (1 shorter events, 0.0 us)
Async XLA Ops:
  102.9 3.3 %copy-start = (f32[1,512,2048]{2,1,0:T(8,128)S(1)}, f32[1,512,2048]{2,1,0:T(8,128)}, u32[]{:S(2)}) copy-start(f32[1,512,2048]{2,1,0:T(8,128)} %get-tuple-element.5) | copy-start | bytes 12582916

commit v2 on v1

v2 whole, which is shorter than its diff:
```python
import functools

import jax
import jax.numpy as jnp
import ml_dtypes
import numpy as np
from jax import lax
from jax.experimental import pallas as pl
from jax.experimental.pallas import tpu as pltpu
from jax.sharding import PartitionSpec as P

MESH = pl.DeviceIdType.MESH
BLOCK = 128
STEPS = 2
TOK = 512
NZ = 8
ROWS = 512
NSUB = 4
SUB = TOK // NSUB
F32 = jnp.float32
BF16 = jnp.bfloat16


def basis_parts():
    k = np.arange(BLOCK, dtype=np.float64)[:, None]
    n = np.arange(BLOCK, dtype=np.float64)[None, :]
    scale = np.where(k == 0, np.sqrt(1.0 / BLOCK), np.sqrt(2.0 / BLOCK))
    table = (scale * np.cos(np.pi * (2.0 * n + 1.0) * k / (2.0 * BLOCK))).T
    high = table.astype(ml_dtypes.bfloat16)
    low = (table - high.astype(np.float64)).astype(ml_dtypes.bfloat16)
    return np.stack([high, low])


def iota(shape, axis):
    return lax.broadcasted_iota(jnp.int32, shape, axis)


def kernel(
    n_rep,
    x_ref, t_ref, w_ref, m_ref, idx_ref, bt_ref,
    w_out, m_out,
    xa, xt, tv, wb, mb, iv, bt, frow, left, prow, lu,
    yp, ys, rl, ef, lx, xr_send, xr_land, rm_send, rm_land, s_send, sn, sall,
    load_sem, pair_send, pair_recv, rs_send, rs_recv, ag_send, ag_recv,
    xr_ssem, xr_rsem, rm_ssem, rm_rsem, sa_ssem, sa_rsem, sp_ssem, sp_rsem,
    pl_ssem, pl_rsem, fw_ssem, fw_rsem, out_sem, outp_ssem, outp_rsem,
):
    r = lax.axis_index("rep")
    me = lax.axis_index("tp")
    z = me // 2
    c = me % 2
    o = 1 - c
    lanes = n_rep * 16
    d = 1 - 2 * c
    partner = {"tp": 2 * z + o}

    def zz(k):
        return lax.rem(z + k + 2 * NZ, NZ)

    long_to = {"tp": 2 * zz(d) + c}
    short_to = {"tp": 2 * zz(-d) + c}

    def remote(src, dst, s, v, dev):
        return pltpu.make_async_remote_copy(
            src_ref=src, dst_ref=dst, send_sem=s, recv_sem=v, device_id=dev, device_id_type=MESH
        )

    def cols(j, h):
        return pl.ds(pl.multiple_of((2 * j + h) * BLOCK, BLOCK), BLOCK)

    half_own = pl.ds(pl.multiple_of(c * ROWS, ROWS), ROWS)
    half_other = pl.ds(pl.multiple_of(o * ROWS, ROWS), ROWS)

    loads = {}

    def load(name, k, src, dst):
        copy = pltpu.make_async_copy(src, dst, load_sem.at[k])
        copy.start()
        loads[name] = copy

    steps_out = (4, -3, 3, -2, 2, -1, 1, 0)
    load("x0", 0, x_ref.at[0], xa.at[0, c])
    for i in range(NZ):
        j = zz(d * steps_out[i])
        load(("w", i), 8 + i, w_ref.at[:, cols(j, c)], wb.at[j, half_own])
    load("ix", 2, idx_ref, iv.at[c])
    load("bt", 1, bt_ref, bt)
    load("x1", 3, x_ref.at[1], xa.at[1, c])
    load("t", 4, t_ref, tv)
    for j in range(NZ):
        load(("m", j), 16 + j, m_ref.at[0, :, pl.ds(2 * BLOCK * j, 2 * BLOCK)], mb.at[j])

    barrier = pltpu.get_barrier_semaphore()
    for k in range(1, 2 * NZ):
        pl.semaphore_signal(barrier, inc=1, device_id={"tp": lax.rem(me + k, 2 * NZ)}, device_id_type=MESH)
    for k in range(1, n_rep):
        pl.semaphore_signal(barrier, inc=1, device_id={"rep": lax.rem(r + k, n_rep)}, device_id_type=MESH)
    pl.semaphore_wait(barrier, 2 * NZ - 1 + n_rep - 1)

    pairs = []

    def pair(k, src, dst):
        copy = remote(src, dst, pair_send.at[k], pair_recv.at[k], partner)
        copy.start()
        pairs.append(copy)

    pair(0, x_ref.at[0], xa.at[0, c])
    for i in range(NZ):
        j = zz(-d * steps_out[i])
        pair(1 + i, w_ref.at[:, cols(j, o)], wb.at[j, half_own])
    pair(9, idx_ref, iv.at[c])
    pair(10, x_ref.at[1], xa.at[1, c])

    order = [(zz(4 * d), zz(-3 * d)), (zz(3 * d), zz(-2 * d)), (zz(2 * d), zz(-d)), (zz(d), z)]

    def forward(s, k):
        p, q = order[k]
        for i in range(2):
            rows = pl.ds(i * 256, 256)
            acc = jnp.zeros((256, 2 * BLOCK), F32)
            for h in range(2):
                w = jnp.concatenate([wb[p, h * ROWS:(h + 1) * ROWS], wb[q, h * ROWS:(h + 1) * ROWS]], axis=1)
                acc += jnp.dot(xa[s, h, rows], w, preferred_element_type=F32)
            yp[2 * k, rows] = acc[:, :BLOCK]
            yp[2 * k + 1, rows] = acc[:, BLOCK:]
            if k == 0:
                ys[s, 0, rows] = acc[:, :BLOCK].astype(BF16)
                ys[s, 1, rows] = acc[:, BLOCK:].astype(BF16)

    def rs_copy(s, way, h, u):
        slot = h - 1 if way == 0 else 3 + h
        rows = pl.ds(u * SUB, SUB)
        if h == 1:
            src = ys.at[s, way, rows]
        else:
            src = rl.at[s, slot - 1, rows]
        return remote(src, rl.at[s, slot, rows], rs_send.at[s, slot, u], rs_recv.at[s, slot, u], (long_to, short_to)[way])

    def rs_first(s):
        for u in range(NSUB):
            for way in range(2):
                rs_copy(s, way, 1, u).start()

    def rs_wave(s, h, u):
        rows = pl.ds(u * SUB, SUB)
        for way in range(2):
            if h > 4 - way:
                continue
            rs_copy(s, way, h - 1, u).wait_recv()
            slot = h - 2 if way == 0 else 2 + h
            rl[s, slot, rows] = (rl[s, slot, rows].astype(F32) + yp[2 * (h - 1) + way, rows]).astype(BF16)
            rs_copy(s, way, h, u).start()

    def rs_last(s, u):
        rows = pl.ds(u * SUB, SUB)
        rs_copy(s, 1, 3, u).wait_recv()
        rs_copy(s, 0, 4, u).wait_recv()
        total = yp[7, rows] + rl[s, 3, rows].astype(F32) + rl[s, 6, rows].astype(F32)
        ef[s, c, z, rows] = (total - tv[s, rows].astype(F32)).astype(BF16)

    def rs_rest(s, work):
        for h in range(2, 5):
            for u in range(NSUB):
                rs_wave(s, h, u)
                run(work, 1)
        for u in range(NSUB):
            rs_last(s, u)
        run(work, len(work))

    def ag_copy(s, way, h, u):
        slot = h - 1 if way == 0 else 3 + h
        rows = pl.ds(u * SUB, SUB)
        origin = zz(-d * (h - 1)) if way == 0 else zz(d * (h - 1))
        block = ef.at[s, c, origin, rows]
        return remote(block, block, ag_send.at[s, slot, u], ag_recv.at[s, slot, u], (long_to, short_to)[way])

    def fw_copy(s, q):
        block = ef.at[s, c, zz(d * q)]
        k = q + 4 if q > -4 else 8
        return remote(block, block, fw_ssem.at[s, k], fw_rsem.at[s, k], partner)

    def fw_arrival(s, q):
        block = ef.at[s, o, zz(d * q)]
        k = 4 - q if q < 4 else 8
        return remote(block, block, fw_ssem.at[s, k], fw_rsem.at[s, k], partner)

    def ag_wave(s, h, u):
        for way in range(2):
            if h > 1 and h <= 5 - way:
                ag_copy(s, way, h - 1, u).wait_recv()
            if h <= 4 - way:
                ag_copy(s, way, h, u).start()
        if u == NSUB - 1:
            if h == 1:
                fw_copy(s, 0).start()
            else:
                fw_copy(s, 1 - h).start()
                if h <= 4:
                    fw_copy(s, h - 1).start()

    def ag_hop(s, h, work=()):
        for u in range(NSUB):
            ag_wave(s, h, u)
            run(work, 1)

    def arrange(s):
        pick = jnp.where(iota((NZ, 16), 1) == 2 * iota((NZ, 16), 0) + c, 1.0, 0.0).astype(BF16)
        half = n_rep * 8
        source = iota((half, lanes), 0)
        place = iota((half, lanes), 1)
        total = jnp.zeros((NZ, lanes), F32)
        for h in range(2):
            turned = lax.dot_general(
                pick, iv[h, s].astype(F32).astype(BF16), (((1,), (1,)), ((), ())), preferred_element_type=F32
            )
            to = jnp.where(place == (source // 8) * 16 + h * 8 + source % 8, 1.0, 0.0).astype(BF16)
            total += jnp.dot(turned.astype(BF16), to, preferred_element_type=F32)
        frow[s] = total

    def build_replicas(s, j):
        onehot = jnp.where(iota((BLOCK, lanes), 0).astype(F32) == frow[s, pl.ds(j, 1)], 1.0, 0.0).astype(BF16)
        kept = jnp.dot(bt[0], onehot, preferred_element_type=F32)
        for a in range(8):
            mine = (iota((BLOCK, lanes), 1) % 16) // 2 == a
            lu[s, j, a * BLOCK:(a + 1) * BLOCK] = jnp.where(mine, kept, 0.0).astype(BF16)

    def build_rows(s):
        lane = iota((lanes, BLOCK), 1)
        own = jnp.where(iota((lanes, BLOCK), 0) == 16 * r + lane % 16, 1.0, 0.0).astype(BF16)
        spread_rows = jnp.dot(frow[s].astype(BF16), own, preferred_element_type=F32)
        flat = jnp.where(iota((NZ, BLOCK), 1) // 16 == iota((NZ, BLOCK), 0), spread_rows, 0.0)
        row = jnp.sum(flat, axis=0, keepdims=True)
        onehot = jnp.where(iota((BLOCK, BLOCK), 0).astype(F32) == row, 1.0, 0.0).astype(BF16)
        kept = jnp.dot(bt[0], onehot, preferred_element_type=F32).T
        out = jnp.zeros((NZ * 16, TOK), F32)
        for h in range(2):
            for a in range(4):
                mine = (iota((BLOCK, BLOCK), 0) % 16) // 2 == 4 * h + a
                lx[:, a * BLOCK:(a + 1) * BLOCK] = jnp.where(mine, kept, 0.0).astype(BF16)
            out += lax.dot_general(lx[...], xa[s, h], (((1,), (1,)), ((), ())), preferred_element_type=F32)
        xr_send[s] = out.astype(BF16).reshape(NZ, 16, TOK)

    def xr_copy(s, k):
        to = zz(k)
        return remote(
            xr_send.at[s, to], xr_land.at[s, z], xr_ssem.at[s, k], xr_rsem.at[s, k], {"tp": 2 * to + c}
        )

    def build_own(s, g):
        mine = iv[c, s, pl.ds(pl.multiple_of(8 * r, 8), 8)].astype(F32).astype(BF16)
        lane = iota((16, BLOCK), 1)
        to = jnp.where(iota((16, BLOCK), 0) == 8 * g + lane // 16, 1.0, 0.0).astype(BF16)
        wide = jnp.dot(mine, to, preferred_element_type=F32)
        flat = jnp.where(iota((8, BLOCK), 1) % 8 == iota((8, BLOCK), 0), wide, 0.0)
        row = jnp.sum(flat, axis=0, keepdims=True)
        lane = iota((BLOCK, BLOCK), 1)
        hit = iota((BLOCK, BLOCK), 0).astype(F32) == row
        even = (lane // 8) % 2 == 0
        high = jnp.where(hit & even, 1.0, 0.0).astype(BF16)
        low = jnp.where(hit & jnp.logical_not(even), 1.0, 0.0).astype(BF16)
        both = jnp.dot(bt[0], high, preferred_element_type=F32) + jnp.dot(bt[1], low, preferred_element_type=F32)
        turned = both.T
        for a in range(4):
            left[s, g, a * BLOCK:(a + 1) * BLOCK] = jnp.where((lane % 8) // 2 == a, both, 0.0).astype(BF16)
            rows = jnp.where((iota((BLOCK, BLOCK), 0) % 8) // 2 == a, turned, 0.0).astype(BF16)
            prow[s, 4 * g:4 * g + 4, :, a * BLOCK:(a + 1) * BLOCK] = rows.reshape(4, 32, BLOCK)

    def project(s, j):
        table = prow[s, j]
        values = mb[j]
        high = values.astype(BF16)
        low = (values - high.astype(F32)).astype(BF16)
        out = jnp.dot(table, high, preferred_element_type=F32) + jnp.dot(table, low, preferred_element_type=F32)
        rm_send[s, j, 0] = out[0:8, :BLOCK] + out[8:16, :BLOCK]
        rm_send[s, j, 1] = out[16:24, BLOCK:] + out[24:32, BLOCK:]

    def rm_copy(s, k):
        to = lax.rem(me + k, 2 * NZ)
        return remote(
            rm_send.at[s, to // 2, to % 2], rm_land.at[s, me], rm_ssem.at[s, k], rm_rsem.at[s, k], {"tp": to}
        )

    def kept_rows(s):
        for k in range(1, NZ):
            xr_copy(s, k).wait_recv()
        for k in range(1, 2 * NZ):
            rm_copy(s, k).wait_recv()
        xr_land[s, z] = xr_send[s, z]
        rm_land[s, me] = rm_send[s, z, c]
        table = xr_land[s].reshape(NZ * 16, TOK)
        out = jnp.dot(table, ef[s, c, z], preferred_element_type=F32) * (1.0 / TOK)
        out += 0.9 * rm_land[s].reshape(NZ * 16, BLOCK)
        s_send[s] = out.astype(BF16).reshape(NZ, 16, BLOCK)

    def sa_copy(s, k):
        to = zz(k)
        return remote(
            s_send.at[s, to], sn.at[s, c, z], sa_ssem.at[s, k], sa_rsem.at[s, k], {"tp": 2 * to + c}
        )

    def sp_copy(s):
        return remote(sn.at[s, c], sn.at[s, c], sp_ssem.at[s], sp_rsem.at[s], partner)

    def pl_copy(s, k):
        return remote(
            sn.at[s, c], sall.at[s, r], pl_ssem.at[s, k], pl_rsem.at[s, k], {"rep": lax.rem(r + k, n_rep)}
        )

    def share(s):
        for k in range(1, NZ):
            sa_copy(s, k).start()
        sn[s, c, z] = s_send[s, z]

    def spread(s):
        for k in range(1, NZ):
            sa_copy(s, k).wait_recv()
        for k in range(1, n_rep):
            pl_copy(s, k).start()
        sp_copy(s).start()
        sall[s, r] = sn[s, c]

    def collect(s):
        for k in range(1, n_rep):
            pl_copy(s, k).wait_recv()

    def update(s, j):
        stack = sall[s, :, j].reshape(lanes, BLOCK)
        for i in range(4):
            rows = pl.ds(i * 256, 256)
            change = jnp.dot(lu[s, j, rows], stack, preferred_element_type=F32)
            wb[j, rows] = (wb[j, rows].astype(F32) - 0.1 * change).astype(BF16)

    def momentum(s, q):
        fw_arrival(s, q).wait_recv()
        j = zz(d * q)
        e = jnp.concatenate([ef[s, 0, j], ef[s, 1, j]], axis=1)
        parts = []
        for h in range(2):
            both = sn[s, h, j].astype(F32)
            parts.append(jnp.where(c == 0, both[:8], both[8:]))
        zero = jnp.zeros((8, BLOCK), F32)
        top = jnp.concatenate([parts[0], zero], axis=1)
        low = jnp.concatenate([zero, parts[1]], axis=1)
        block = jnp.concatenate([top, top, low, low], axis=0)
        right = jnp.concatenate([jnp.where(j % 4 == i, block, 0.0) for i in range(4)], axis=0).astype(BF16)
        for i in range(2):
            rows = pl.ds(i * 256, 256)
            grad = jnp.dot(xt[s, rows], e, preferred_element_type=F32)
            taken = jnp.dot(left[s, j // 4, rows], right, preferred_element_type=F32)
            mb[j, rows] = 0.9 * mb[j, rows] + grad * (1.0 / TOK) - taken

    def gain(q):
        momentum(0, q)
        project(1, zz(d * q))

    def finish(q):
        momentum(1, q)
        j = zz(d * q)
        m_copy(j).start()

    def m_copy(j):
        columns = pl.ds(pl.multiple_of(2 * BLOCK * j, 2 * BLOCK), 2 * BLOCK)
        return pltpu.make_async_copy(mb.at[j], m_out.at[0, :, columns], out_sem.at[NZ + j])

    def run(work, count):
        for _ in range(min(count, len(work))):
            work.pop(0)()

    def turn(s):
        xt[s] = xa[s, c].T

    loads["x0"].wait()
    pairs[0].wait_recv()

    def ready(k):
        for i in (2 * k, 2 * k + 1):
            loads["w", i].wait()
            pairs[1 + i].wait_recv()

    ready(0)
    forward(0, 0)
    rs_first(0)
    ready(1)
    forward(0, 1)
    loads["bt"].wait()
    loads["ix"].wait()
    pairs[9].wait_recv()
    arrange(0)
    build_rows(0)
    for k in range(1, NZ):
        xr_copy(0, k).start()
    ready(2)
    ready(3)

    def first_products():
        for j in range(NZ):
            loads["m", j].wait()
        project(0, 0)

    def send_products(s):
        for k in range(1, 2 * NZ):
            rm_copy(s, k).start()

    def last_products():
        project(0, 7)
        send_products(0)

    def second_rows():
        loads["x1"].wait()
        pairs[10].wait_recv()
        arrange(1)
        build_rows(1)

    def two(f, s, j):
        return lambda: (f(s, j), f(s, j + 1))

    rs_rest(0, [
        lambda: forward(0, 2),
        lambda: build_own(0, 0),
        lambda: (build_own(0, 1), loads["t"].wait()),
        lambda: forward(0, 3),
        first_products,
        lambda: (project(0, 1), project(0, 2)),
        lambda: (project(0, 3), project(0, 4)),
        lambda: (project(0, 5), project(0, 6)),
        last_products,
        two(build_replicas, 0, 0),
        two(build_replicas, 0, 2),
        two(build_replicas, 0, 4),
    ])
    kept_rows(0)
    share(0)
    ag_hop(0, 1)
    two(build_replicas, 0, 6)()
    turn(0)
    second_rows()
    spread(0)
    ag_hop(0, 2)
    for k in range(1, NZ):
        xr_copy(1, k).start()
    build_own(1, 0)
    build_own(1, 1)
    sp_copy(0).wait_recv()
    gain(0)
    ag_hop(0, 3)
    collect(0)

    for k in range(4):
        update(0, order[k][0])
        update(0, order[k][1])
        forward(1, k)
        if k == 0:
            rs_first(1)
        if k == 1:
            ag_hop(0, 4)

    def last_gain():
        gain(4)
        send_products(1)

    rs_rest(1, [
        lambda: gain(1),
        lambda: gain(-1),
        lambda: gain(2),
        lambda: gain(-2),
        lambda: (ag_hop(0, 5), gain(3)),
        lambda: gain(-3),
        last_gain,
        lambda: turn(1),
        two(build_replicas, 1, 0),
        two(build_replicas, 1, 2),
        two(build_replicas, 1, 4),
        two(build_replicas, 1, 6),
    ])
    kept_rows(1)
    share(1)
    ag_hop(1, 1)
    spread(1)
    ag_hop(1, 2)
    sp_copy(1).wait_recv()
    ag_hop(1, 3, [lambda: finish(0), lambda: finish(1), lambda: finish(-1)])
    collect(1)
    out_copies = []

    def new_weight(j):
        update(1, j)
        own = pltpu.make_async_copy(wb.at[j, half_own], w_out.at[:, cols(j, c)], out_sem.at[j])
        own.start()
        other = remote(wb.at[j, half_other], w_out.at[:, cols(j, c)], outp_ssem.at[j], outp_rsem.at[j], partner)
        other.start()
        out_copies.extend([own, other])

    new_weights = [lambda j=j: new_weight(j) for j in range(NZ)]
    ag_hop(1, 4, new_weights)
    ag_hop(1, 5, new_weights)
    finish(2)
    finish(-2)
    finish(3)
    finish(-3)
    finish(4)

    for copy in out_copies:
        copy.wait()
    for j in range(NZ):
        m_copy(j).wait()
    for copy in pairs:
        copy.wait_send()
    for s in range(STEPS):
        for way in range(2):
            for h in range(1, 5 - way):
                for u in range(NSUB):
                    rs_copy(s, way, h, u).wait_send()
                    ag_copy(s, way, h, u).wait_send()
        for q in range(-4, 4):
            fw_copy(s, q).wait_send()
        for k in range(1, NZ):
            xr_copy(s, k).wait_send()
            sa_copy(s, k).wait_send()
        for k in range(1, 2 * NZ):
            rm_copy(s, k).wait_send()
        for k in range(1, n_rep):
            pl_copy(s, k).wait_send()
        sp_copy(s).wait_send()


def local(n_rep, inputs, targets, weight, momentum, indices):
    lanes = n_rep * 16
    arranged = indices.transpose(0, 1, 2, 4, 3).reshape(STEPS, n_rep * 8, 2 * NZ)
    any_space = pl.BlockSpec(memory_space=pl.ANY)
    dma = pltpu.SemaphoreType.DMA
    scratch = [
        pltpu.VMEM((STEPS, 2, TOK, ROWS), BF16),
        pltpu.VMEM((STEPS, ROWS, TOK), BF16),
        pltpu.VMEM((STEPS, TOK, BLOCK), BF16),
        pltpu.VMEM((NZ, 2 * ROWS, BLOCK), BF16),
        pltpu.VMEM((NZ, ROWS, 2 * BLOCK), F32),
        pltpu.VMEM((2, STEPS, n_rep * 8, 2 * NZ), jnp.int32),
        pltpu.VMEM((2, BLOCK, BLOCK), BF16),
        pltpu.VMEM((STEPS, NZ, lanes), F32),
        pltpu.VMEM((STEPS, 2, ROWS, BLOCK), BF16),
        pltpu.VMEM((STEPS, NZ, 32, ROWS), BF16),
        pltpu.VMEM((STEPS, NZ, 2 * ROWS, lanes), BF16),
        pltpu.VMEM((NZ, TOK, BLOCK), F32),
        pltpu.VMEM((STEPS, 2, TOK, BLOCK), BF16),
        pltpu.VMEM((STEPS, 7, TOK, BLOCK), BF16),
        pltpu.VMEM((STEPS, 2, NZ, TOK, BLOCK), BF16),
        pltpu.VMEM((BLOCK, ROWS), BF16),
        pltpu.VMEM((STEPS, NZ, 16, TOK), BF16),
        pltpu.VMEM((STEPS, NZ, 16, TOK), BF16),
        pltpu.VMEM((STEPS, NZ, 2, 8, BLOCK), F32),
        pltpu.VMEM((STEPS, 2 * NZ, 8, BLOCK), F32),
        pltpu.VMEM((STEPS, NZ, 16, BLOCK), BF16),
        pltpu.VMEM((STEPS, 2, NZ, 16, BLOCK), BF16),
        pltpu.VMEM((STEPS, n_rep, NZ, 16, BLOCK), BF16),
        dma((24,)), dma((11,)), dma((11,)),
        dma((STEPS, 7, NSUB)), dma((STEPS, 7, NSUB)), dma((STEPS, 7, NSUB)), dma((STEPS, 7, NSUB)),
        dma((STEPS, NZ)), dma((STEPS, NZ)), dma((STEPS, 2 * NZ)), dma((STEPS, 2 * NZ)),
        dma((STEPS, NZ)), dma((STEPS, NZ)), dma((STEPS,)), dma((STEPS,)),
        dma((STEPS, n_rep)), dma((STEPS, n_rep)), dma((STEPS, NZ + 1)), dma((STEPS, NZ + 1)),
        dma((2 * NZ,)), dma((NZ,)), dma((NZ,)),
    ]
    return pl.pallas_call(
        functools.partial(kernel, n_rep),
        out_shape=(
            jax.ShapeDtypeStruct(weight.shape, BF16),
            jax.ShapeDtypeStruct(momentum.shape, F32),
        ),
        in_specs=[pl.BlockSpec(memory_space=pltpu.HBM)] * 6,
        out_specs=(any_space, any_space),
        scratch_shapes=scratch,
        compiler_params=pltpu.CompilerParams(
            collective_id=0, has_side_effects=True, vmem_limit_bytes=40 << 20
        ),
    )(inputs, targets, weight, momentum, arranged, jnp.asarray(basis_parts()))


def solution(mesh):
    in_specs = (
        P(None, "rep", "tp"),
        P(None, "rep", "tp"),
        P("tp", None),
        P("rep", "tp", None),
        P(None, None, "tp", None, None),
    )
    out_specs = (P("tp", None), P("rep", "tp", None))
    return jax.shard_map(
        functools.partial(local, mesh.shape["rep"]), mesh=mesh, in_specs=in_specs, out_specs=out_specs, check_vma=False
    )
```

time: 108 us -> 98.4 us (0.911)
  Pallas kernels: 99.8 us -> 86.4 us
  local copies, waits for them, and re-layouts: 7.07 us -> 11 us
    pallas_call x1, Pallas kernels: 99.8 us -> 86.4 us  [local(): pl.pallas_call(functools.partial(kernel, n_rep), out_shape=(jax.ShapeDtyp...]
    unnamed x5 -> x14, local copies, waits for them, and re-layouts: 6.33 us -> 11 us
where the time goes in v2:
time: 98.4 us; the launch traced here: 98.1 us
  Pallas kernels  86.4 us (88%)
  local copies, waits for them, and re-layouts  11 us (11%)
    pallas_call x1, Pallas kernels, local(): pl.pallas_call(functools.partial(kernel, n_rep), out_shape=(jax.ShapeDtyp...  86.4 us
    unnamed x14, local copies, waits for them, and re-layouts  11 us

profile of v2, /device:TPU:1, one launch (start us, length us, event | category | flops | bytes accessed | tf_op | source)
XLA Modules:
  0.0 98.1 jit_solution(2908771600689964120)
XLA Ops:
  0.6 0.0 copy-start
  0.6 2.2 %copy-done = f32[1,512,2048]{2,1,0:T(8,128)S(1)} copy-done((f32[1,512,2048]{2,1,0:T(8,128)S(1)}, f32[1,512,2048]{2,1,0:T(8,128)}, u32[]{:S(2)}) %copy-start) | copy-done | bytes 4194328
  2.8 0.0 copy-start.1
  2.8 1.6 %copy-done.1 = bf16[512,2048]{1,0:T(8,128)(2,1)S(1)} copy-done((bf16[512,2048]{1,0:T(8,128)(2,1)S(1)}, bf16[512,2048]{1,0:T(8,128)(2,1)}, u32[]{:S(2)}) %copy-start.1) | copy-done | bytes 2097176
  4.4 0.0 copy-start.2
  4.4 1.2 %copy-done.2 = bf16[2,512,512]{2,1,0:T(8,128)(2,1)S(1)} copy-done((bf16[2,512,512]{2,1,0:T(8,128)(2,1)S(1)}, bf16[2,512,512]{2,1,0:T(8,128)(2,1)}, u32[]{:S(2)}) %copy-start.2) | copy-done | bytes 1048600
  5.6 0.0 copy-start.3
  5.6 0.9 copy-done.3
  6.6 0.0 copy-start.4
  6.6 0.9 copy-done.4
  7.5 0.0 copy-start.5
  7.5 0.8 copy-done.5
  8.3 86.4 %shard_map.77 = (bf16[512,2048]{1,0:T(8,128)(2,1)S(1)}, f32[1,512,2048]{2,1,0:T(8,128)S(1)}) custom-call(bf16[2,512,512]{2,1,0:T(8,128)(2,1)S(1)} %copy-done.2, bf16[2,512,128]{2,1,0:T(8,128)(2,1)S(1)} %copy-done.3, bf16[512,2048]{1,0:T(8,128)(2,1)S(1)} %copy-done.1, f32[1,512,2048]{2,1,0:T(8,128)S(1)} %copy-done, s32[2,128,16]{2,1,0:T(8,128)S(1)} %bitcast.3, ...), custom_call_target="tpu_custom_call" | custom-call | tf_op jit(solution)/shard_map/pallas_call | solution.py:562
  94.8 1.3 %copy.10 = bf16[512,2048]{1,0:T(8,128)(2,1)} copy(bf16[512,2048]{1,0:T(8,128)(2,1)S(1)} %get-tuple-element.4) | data formatting | bytes 4194304
  96.1 2.0 %copy.11 = f32[1,512,2048]{2,1,0:T(8,128)} copy(f32[1,512,2048]{2,1,0:T(8,128)S(1)} %get-tuple-element.5) | data formatting | bytes 8388608
Async XLA Ops:
  0.6 2.2 %copy-start = (f32[1,512,2048]{2,1,0:T(8,128)S(1)}, f32[1,512,2048]{2,1,0:T(8,128)}, u32[]{:S(2)}) copy-start(f32[1,512,2048]{2,1,0:T(8,128)} %m_ref.1) | copy-start | bytes 12582916
  2.8 1.6 %copy-start.1 = (bf16[512,2048]{1,0:T(8,128)(2,1)S(1)}, bf16[512,2048]{1,0:T(8,128)(2,1)}, u32[]{:S(2)}) copy-start(bf16[512,2048]{1,0:T(8,128)(2,1)} %w_ref.1) | copy-start | bytes 6291460
  4.4 1.2 %copy-start.2 = (bf16[2,512,512]{2,1,0:T(8,128)(2,1)S(1)}, bf16[2,512,512]{2,1,0:T(8,128)(2,1)}, u32[]{:S(2)}) copy-start(bf16[2,512,512]{2,1,0:T(8,128)(2,1)} %x_ref.1) | copy-start | bytes 3145732
  5.6 0.9 copy-start.3
  6.6 0.9 copy-start.4
  7.5 0.8 copy-start.5

commit v3 on v2

--- a/solution.py
+++ b/solution.py
@@ -16,6 +16,7 @@
 NZ = 8
 ROWS = 512
 NSUB = 4
+SIDE = 4
 SUB = TOK // NSUB
 F32 = jnp.float32
 BF16 = jnp.bfloat16
@@ -43,7 +44,7 @@
     yp, ys, rl, ef, lx, xr_send, xr_land, rm_send, rm_land, s_send, sn, sall,
     load_sem, pair_send, pair_recv, rs_send, rs_recv, ag_send, ag_recv,
     xr_ssem, xr_rsem, rm_ssem, rm_rsem, sa_ssem, sa_rsem, sp_ssem, sp_rsem,
-    pl_ssem, pl_rsem, fw_ssem, fw_rsem, out_sem, outp_ssem, outp_rsem,
+    pl_ssem, pl_rsem, fw_ssem, fw_rsem, out_sem, outp_ssem, outp_rsem, token,
 ):
     r = lax.axis_index("rep")
     me = lax.axis_index("tp")
@@ -71,6 +72,24 @@
     half_own = pl.ds(pl.multiple_of(c * ROWS, ROWS), ROWS)
     half_other = pl.ds(pl.multiple_of(o * ROWS, ROWS), ROWS)
 
+    side = SIDE
+    along_x = [{"rep": (r // side) * side + lax.rem(r + k, side)} for k in (1, side - 1)]
+    along_y = [{"rep": lax.rem(r + k * side, n_rep)} for k in (1, side - 1)]
+    along_z = [long_to, short_to]
+    if n_rep != side * side:
+        along_x, along_y = [], []
+    barrier = pltpu.get_barrier_semaphore()
+    for peer in [partner] + along_z + along_x + along_y:
+        pl.semaphore_signal(barrier, inc=1, device_id=peer, device_id_type=MESH)
+
+    def tell(k, peers):
+        for peer in peers:
+            pl.semaphore_signal(token.at[k], inc=1, device_id=peer, device_id_type=MESH)
+
+    def told(k, peers):
+        if peers:
+            pl.semaphore_wait(token.at[k], len(peers))
+
     loads = {}
 
     def load(name, k, src, dst):
@@ -79,172 +98,16 @@
         loads[name] = copy
 
     steps_out = (4, -3, 3, -2, 2, -1, 1, 0)
+    load("ix", 2, idx_ref, iv.at[c])
+    load("bt", 1, bt_ref, bt)
     load("x0", 0, x_ref.at[0], xa.at[0, c])
     for i in range(NZ):
         j = zz(d * steps_out[i])
         load(("w", i), 8 + i, w_ref.at[:, cols(j, c)], wb.at[j, half_own])
-    load("ix", 2, idx_ref, iv.at[c])
-    load("bt", 1, bt_ref, bt)
     load("x1", 3, x_ref.at[1], xa.at[1, c])
     load("t", 4, t_ref, tv)
     for j in range(NZ):
         load(("m", j), 16 + j, m_ref.at[0, :, pl.ds(2 * BLOCK * j, 2 * BLOCK)], mb.at[j])
-
-    barrier = pltpu.get_barrier_semaphore()
-    for k in range(1, 2 * NZ):
-        pl.semaphore_signal(barrier, inc=1, device_id={"tp": lax.rem(me + k, 2 * NZ)}, device_id_type=MESH)
-    for k in range(1, n_rep):
-        pl.semaphore_signal(barrier, inc=1, device_id={"rep": lax.rem(r + k, n_rep)}, device_id_type=MESH)
-    pl.semaphore_wait(barrier, 2 * NZ - 1 + n_rep - 1)
-
-    pairs = []
-
-    def pair(k, src, dst):
-        copy = remote(src, dst, pair_send.at[k], pair_recv.at[k], partner)
-        copy.start()
-        pairs.append(copy)
-
-    pair(0, x_ref.at[0], xa.at[0, c])
-    for i in range(NZ):
-        j = zz(-d * steps_out[i])
-        pair(1 + i, w_ref.at[:, cols(j, o)], wb.at[j, half_own])
-    pair(9, idx_ref, iv.at[c])
-    pair(10, x_ref.at[1], xa.at[1, c])
-
-    order = [(zz(4 * d), zz(-3 * d)), (zz(3 * d), zz(-2 * d)), (zz(2 * d), zz(-d)), (zz(d), z)]
-
-    def forward(s, k):
-        p, q = order[k]
-        for i in range(2):
-            rows = pl.ds(i * 256, 256)
-            acc = jnp.zeros((256, 2 * BLOCK), F32)
-            for h in range(2):
-                w = jnp.concatenate([wb[p, h * ROWS:(h + 1) * ROWS], wb[q, h * ROWS:(h + 1) * ROWS]], axis=1)
-                acc += jnp.dot(xa[s, h, rows], w, preferred_element_type=F32)
-            yp[2 * k, rows] = acc[:, :BLOCK]
-            yp[2 * k + 1, rows] = acc[:, BLOCK:]
-            if k == 0:
-                ys[s, 0, rows] = acc[:, :BLOCK].astype(BF16)
-                ys[s, 1, rows] = acc[:, BLOCK:].astype(BF16)
-
-    def rs_copy(s, way, h, u):
-        slot = h - 1 if way == 0 else 3 + h
-        rows = pl.ds(u * SUB, SUB)
-        if h == 1:
-            src = ys.at[s, way, rows]
-        else:
-            src = rl.at[s, slot - 1, rows]
-        return remote(src, rl.at[s, slot, rows], rs_send.at[s, slot, u], rs_recv.at[s, slot, u], (long_to, short_to)[way])
-
-    def rs_first(s):
-        for u in range(NSUB):
-            for way in range(2):
-                rs_copy(s, way, 1, u).start()
-
-    def rs_wave(s, h, u):
-        rows = pl.ds(u * SUB, SUB)
-        for way in range(2):
-            if h > 4 - way:
-                continue
-            rs_copy(s, way, h - 1, u).wait_recv()
-            slot = h - 2 if way == 0 else 2 + h
-            rl[s, slot, rows] = (rl[s, slot, rows].astype(F32) + yp[2 * (h - 1) + way, rows]).astype(BF16)
-            rs_copy(s, way, h, u).start()
-
-    def rs_last(s, u):
-        rows = pl.ds(u * SUB, SUB)
-        rs_copy(s, 1, 3, u).wait_recv()
-        rs_copy(s, 0, 4, u).wait_recv()
-        total = yp[7, rows] + rl[s, 3, rows].astype(F32) + rl[s, 6, rows].astype(F32)
-        ef[s, c, z, rows] = (total - tv[s, rows].astype(F32)).astype(BF16)
-
-    def rs_rest(s, work):
-        for h in range(2, 5):
-            for u in range(NSUB):
-                rs_wave(s, h, u)
-                run(work, 1)
-        for u in range(NSUB):
-            rs_last(s, u)
-        run(work, len(work))
-
-    def ag_copy(s, way, h, u):
-        slot = h - 1 if way == 0 else 3 + h
-        rows = pl.ds(u * SUB, SUB)
-        origin = zz(-d * (h - 1)) if way == 0 else zz(d * (h - 1))
-        block = ef.at[s, c, origin, rows]
-        return remote(block, block, ag_send.at[s, slot, u], ag_recv.at[s, slot, u], (long_to, short_to)[way])
-
-    def fw_copy(s, q):
-        block = ef.at[s, c, zz(d * q)]
-        k = q + 4 if q > -4 else 8
-        return remote(block, block, fw_ssem.at[s, k], fw_rsem.at[s, k], partner)
-
-    def fw_arrival(s, q):
-        block = ef.at[s, o, zz(d * q)]
-        k = 4 - q if q < 4 else 8
-        return remote(block, block, fw_ssem.at[s, k], fw_rsem.at[s, k], partner)
-
-    def ag_wave(s, h, u):
-        for way in range(2):
-            if h > 1 and h <= 5 - way:
-                ag_copy(s, way, h - 1, u).wait_recv()
-            if h <= 4 - way:
-                ag_copy(s, way, h, u).start()
-        if u == NSUB - 1:
-            if h == 1:
-                fw_copy(s, 0).start()
-            else:
-                fw_copy(s, 1 - h).start()
-                if h <= 4:
-                    fw_copy(s, h - 1).start()
-
-    def ag_hop(s, h, work=()):
-        for u in range(NSUB):
-            ag_wave(s, h, u)
-            run(work, 1)
-
-    def arrange(s):
-        pick = jnp.where(iota((NZ, 16), 1) == 2 * iota((NZ, 16), 0) + c, 1.0, 0.0).astype(BF16)
-        half = n_rep * 8
-        source = iota((half, lanes), 0)
-        place = iota((half, lanes), 1)
-        total = jnp.zeros((NZ, lanes), F32)
-        for h in range(2):
-            turned = lax.dot_general(
-                pick, iv[h, s].astype(F32).astype(BF16), (((1,), (1,)), ((), ())), preferred_element_type=F32
-            )
-            to = jnp.where(place == (source // 8) * 16 + h * 8 + source % 8, 1.0, 0.0).astype(BF16)
-            total += jnp.dot(turned.astype(BF16), to, preferred_element_type=F32)
-        frow[s] = total
-
-    def build_replicas(s, j):
-        onehot = jnp.where(iota((BLOCK, lanes), 0).astype(F32) == frow[s, pl.ds(j, 1)], 1.0, 0.0).astype(BF16)
-        kept = jnp.dot(bt[0], onehot, preferred_element_type=F32)
-        for a in range(8):
-            mine = (iota((BLOCK, lanes), 1) % 16) // 2 == a
-            lu[s, j, a * BLOCK:(a + 1) * BLOCK] = jnp.where(mine, kept, 0.0).astype(BF16)
-
-    def build_rows(s):
-        lane = iota((lanes, BLOCK), 1)
-        own = jnp.where(iota((lanes, BLOCK), 0) == 16 * r + lane % 16, 1.0, 0.0).astype(BF16)
-        spread_rows = jnp.dot(frow[s].astype(BF16), own, preferred_element_type=F32)
-        flat = jnp.where(iota((NZ, BLOCK), 1) // 16 == iota((NZ, BLOCK), 0), spread_rows, 0.0)
-        row = jnp.sum(flat, axis=0, keepdims=True)
-        onehot = jnp.where(iota((BLOCK, BLOCK), 0).astype(F32) == row, 1.0, 0.0).astype(BF16)
-        kept = jnp.dot(bt[0], onehot, preferred_element_type=F32).T
-        out = jnp.zeros((NZ * 16, TOK), F32)
-        for h in range(2):
-            for a in range(4):
-                mine = (iota((BLOCK, BLOCK), 0) % 16) // 2 == 4 * h + a
-                lx[:, a * BLOCK:(a + 1) * BLOCK] = jnp.where(mine, kept, 0.0).astype(BF16)
-            out += lax.dot_general(lx[...], xa[s, h], (((1,), (1,)), ((), ())), preferred_element_type=F32)
-        xr_send[s] = out.astype(BF16).reshape(NZ, 16, TOK)
-
-    def xr_copy(s, k):
-        to = zz(k)
-        return remote(
-            xr_send.at[s, to], xr_land.at[s, z], xr_ssem.at[s, k], xr_rsem.at[s, k], {"tp": 2 * to + c}
-        )
 
     def build_own(s, g):
         mine = iv[c, s, pl.ds(pl.multiple_of(8 * r, 8), 8)].astype(F32).astype(BF16)
@@ -274,6 +137,167 @@
         rm_send[s, j, 0] = out[0:8, :BLOCK] + out[8:16, :BLOCK]
         rm_send[s, j, 1] = out[16:24, BLOCK:] + out[24:32, BLOCK:]
 
+    def early():
+        loads["bt"].wait()
+        loads["ix"].wait()
+        build_own(0, 0)
+        build_own(0, 1)
+
+    early()
+    pl.semaphore_wait(barrier, 1 + len(along_z + along_x + along_y))
+    tell(0, along_z)
+    tell(3, along_x)
+
+    pairs = []
+
+    def pair(k, src, dst):
+        copy = remote(src, dst, pair_send.at[k], pair_recv.at[k], partner)
+        copy.start()
+        pairs.append(copy)
+
+    pair(9, idx_ref, iv.at[c])
+    pair(0, x_ref.at[0], xa.at[0, c])
+    for i in range(NZ):
+        j = zz(-d * steps_out[i])
+        pair(1 + i, w_ref.at[:, cols(j, o)], wb.at[j, half_own])
+    pair(10, x_ref.at[1], xa.at[1, c])
+
+    order = [(zz(4 * d), zz(-3 * d)), (zz(3 * d), zz(-2 * d)), (zz(2 * d), zz(-d)), (zz(d), z)]
+
+    def forward(s, k):
+        p, q = order[k]
+        for i in range(2):
+            rows = pl.ds(i * 256, 256)
+            acc = jnp.zeros((256, 2 * BLOCK), F32)
+            for h in range(2):
+                w = jnp.concatenate([wb[p, h * ROWS:(h + 1) * ROWS], wb[q, h * ROWS:(h + 1) * ROWS]], axis=1)
+                acc += jnp.dot(xa[s, h, rows], w, preferred_element_type=F32)
+            yp[2 * k, rows] = acc[:, :BLOCK]
+            yp[2 * k + 1, rows] = acc[:, BLOCK:]
+            if k == 0:
+                ys[s, 0, rows] = acc[:, :BLOCK].astype(BF16)
+                ys[s, 1, rows] = acc[:, BLOCK:].astype(BF16)
+
+    def rs_copy(s, way, h, u):
+        slot = h - 1 if way == 0 else 3 + h
+        rows = pl.ds(u * SUB, SUB)
+        if h == 1:
+            src = ys.at[s, way, rows]
+        else:
+            src = rl.at[s, slot - 1, rows]
+        return remote(src, rl.at[s, slot, rows], rs_send.at[s, slot, u], rs_recv.at[s, slot, u], (long_to, short_to)[way])
+
+    def rs_first(s):
+        for u in range(NSUB):
+            for way in range(2):
+                rs_copy(s, way, 1, u).start()
+
+    def rs_wave(s, h, u):
+        rows = pl.ds(u * SUB, SUB)
+        for way in range(2):
+            if h > 4 - way:
+                continue
+            rs_copy(s, way, h - 1, u).wait_recv()
+            slot = h - 2 if way == 0 else 2 + h
+            rl[s, slot, rows] = (rl[s, slot, rows].astype(F32) + yp[2 * (h - 1) + way, rows]).astype(BF16)
+            rs_copy(s, way, h, u).start()
+
+    def rs_last(s, u):
+        rows = pl.ds(u * SUB, SUB)
+        rs_copy(s, 1, 3, u).wait_recv()
+        rs_copy(s, 0, 4, u).wait_recv()
+        total = yp[7, rows] + rl[s, 3, rows].astype(F32) + rl[s, 6, rows].astype(F32)
+        ef[s, c, z, rows] = (total - tv[s, rows].astype(F32)).astype(BF16)
+
+    def rs_rest(s, work):
+        for h in range(2, 5):
+            for u in range(NSUB):
+                rs_wave(s, h, u)
+                run(work, (len(work) + NSUB * (5 - h) - u - 1) // (NSUB * (5 - h) - u))
+        for u in range(NSUB):
+            rs_last(s, u)
+            if u < NSUB - 1:
+                ag_wave(s, 1, u)
+
+    def ag_copy(s, way, h, u):
+        slot = h - 1 if way == 0 else 3 + h
+        rows = pl.ds(u * SUB, SUB)
+        origin = zz(-d * (h - 1)) if way == 0 else zz(d * (h - 1))
+        block = ef.at[s, c, origin, rows]
+        return remote(block, block, ag_send.at[s, slot, u], ag_recv.at[s, slot, u], (long_to, short_to)[way])
+
+    def fw_copy(s, q):
+        block = ef.at[s, c, zz(d * q)]
+        k = q + 4 if q > -4 else 8
+        return remote(block, block, fw_ssem.at[s, k], fw_rsem.at[s, k], partner)
+
+    def fw_arrival(s, q):
+        block = ef.at[s, o, zz(d * q)]
+        k = 4 - q if q < 4 else 8
+        return remote(block, block, fw_ssem.at[s, k], fw_rsem.at[s, k], partner)
+
+    def ag_wave(s, h, u):
+        for way in range(2):
+            if h > 1 and h <= 5 - way:
+                ag_copy(s, way, h - 1, u).wait_recv()
+            if h <= 4 - way:
+                ag_copy(s, way, h, u).start()
+        if u == NSUB - 1:
+            if h == 1:
+                fw_copy(s, 0).start()
+            else:
+                fw_copy(s, 1 - h).start()
+                if h <= 4:
+                    fw_copy(s, h - 1).start()
+
+    def ag_hop(s, h, work=(), low=0, high=NSUB):
+        for u in range(low, high):
+            ag_wave(s, h, u)
+            run(work, (len(work) + high - u - 1) // (high - u))
+
+    def arrange(s):
+        pick = jnp.where(iota((NZ, 16), 1) == 2 * iota((NZ, 16), 0) + c, 1.0, 0.0).astype(BF16)
+        half = n_rep * 8
+        source = iota((half, lanes), 0)
+        place = iota((half, lanes), 1)
+        total = jnp.zeros((NZ, lanes), F32)
+        for h in range(2):
+            turned = lax.dot_general(
+                pick, iv[h, s].astype(F32).astype(BF16), (((1,), (1,)), ((), ())), preferred_element_type=F32
+            )
+            to = jnp.where(place == (source // 8) * 16 + h * 8 + source % 8, 1.0, 0.0).astype(BF16)
+            total += jnp.dot(turned.astype(BF16), to, preferred_element_type=F32)
+        frow[s] = total
+
+    def build_replicas(s, j):
+        onehot = jnp.where(iota((BLOCK, lanes), 0).astype(F32) == frow[s, pl.ds(j, 1)], 1.0, 0.0).astype(BF16)
+        kept = jnp.dot(bt[0], onehot, preferred_element_type=F32)
+        for a in range(8):
+            mine = (iota((BLOCK, lanes), 1) % 16) // 2 == a
+            lu[s, j, a * BLOCK:(a + 1) * BLOCK] = jnp.where(mine, kept, 0.0).astype(BF16)
+
+    def build_rows(s):
+        lane = iota((lanes, BLOCK), 1)
+        own = jnp.where(iota((lanes, BLOCK), 0) == 16 * r + lane % 16, 1.0, 0.0).astype(BF16)
+        spread_rows = jnp.dot(frow[s].astype(BF16), own, preferred_element_type=F32)
+        flat = jnp.where(iota((NZ, BLOCK), 1) // 16 == iota((NZ, BLOCK), 0), spread_rows, 0.0)
+        row = jnp.sum(flat, axis=0, keepdims=True)
+        onehot = jnp.where(iota((BLOCK, BLOCK), 0).astype(F32) == row, 1.0, 0.0).astype(BF16)
+        kept = jnp.dot(bt[0], onehot, preferred_element_type=F32).T
+        out = jnp.zeros((NZ * 16, TOK), F32)
+        for h in range(2):
+            for a in range(4):
+                mine = (iota((BLOCK, BLOCK), 0) % 16) // 2 == 4 * h + a
+                lx[:, a * BLOCK:(a + 1) * BLOCK] = jnp.where(mine, kept, 0.0).astype(BF16)
+            out += lax.dot_general(lx[...], xa[s, h], (((1,), (1,)), ((), ())), preferred_element_type=F32)
+        xr_send[s] = out.astype(BF16).reshape(NZ, 16, TOK)
+
+    def xr_copy(s, k):
+        to = zz(k)
+        return remote(
+            xr_send.at[s, to], xr_land.at[s, z], xr_ssem.at[s, k], xr_rsem.at[s, k], {"tp": 2 * to + c}
+        )
+
     def rm_copy(s, k):
         to = lax.rem(me + k, 2 * NZ)
         return remote(
@@ -370,40 +394,43 @@
         xt[s] = xa[s, c].T
 
     loads["x0"].wait()
-    pairs[0].wait_recv()
+    pairs[1].wait_recv()
 
     def ready(k):
         for i in (2 * k, 2 * k + 1):
             loads["w", i].wait()
-            pairs[1 + i].wait_recv()
+            pairs[2 + i].wait_recv()
 
     ready(0)
     forward(0, 0)
     rs_first(0)
     ready(1)
     forward(0, 1)
-    loads["bt"].wait()
-    loads["ix"].wait()
-    pairs[9].wait_recv()
+    pairs[0].wait_recv()
+    told(0, along_z)
+    tell(1, along_z)
     arrange(0)
     build_rows(0)
-    for k in range(1, NZ):
-        xr_copy(0, k).start()
+    told(1, along_z)
+    tell(2, along_z)
     ready(2)
     ready(3)
 
-    def first_products():
-        for j in range(NZ):
-            loads["m", j].wait()
-        project(0, 0)
+    def send_rows():
+        told(2, along_z)
+        for k in range(1, NZ):
+            xr_copy(0, k).start()
+
+    def pass_on(k, before, after):
+        def act():
+            told(k, before)
+            tell(k + 1, after)
+
+        return act
 
     def send_products(s):
         for k in range(1, 2 * NZ):
             rm_copy(s, k).start()
-
-    def last_products():
-        project(0, 7)
-        send_products(0)
 
     def second_rows():
         loads["x1"].wait()
@@ -414,28 +441,35 @@
     def two(f, s, j):
         return lambda: (f(s, j), f(s, j + 1))
 
+    def products(first):
+        def some():
+            for j in (first, first + 1):
+                loads["m", j].wait()
+                project(0, j)
+
+        return some
+
     rs_rest(0, [
         lambda: forward(0, 2),
-        lambda: build_own(0, 0),
-        lambda: (build_own(0, 1), loads["t"].wait()),
+        lambda: (products(0)(), send_rows()),
+        lambda: (products(2)(), pass_on(3, along_x, along_y)()),
         lambda: forward(0, 3),
-        first_products,
-        lambda: (project(0, 1), project(0, 2)),
-        lambda: (project(0, 3), project(0, 4)),
-        lambda: (project(0, 5), project(0, 6)),
-        last_products,
-        two(build_replicas, 0, 0),
+        products(4),
+        products(6),
+        lambda: (send_products(0), loads["t"].wait()),
+        lambda: turn(0),
+        lambda: (two(build_replicas, 0, 0)(), pass_on(4, along_y, along_y)()),
         two(build_replicas, 0, 2),
         two(build_replicas, 0, 4),
+        lambda: (two(build_replicas, 0, 6)(), told(5, along_y)),
     ])
     kept_rows(0)
     share(0)
-    ag_hop(0, 1)
-    two(build_replicas, 0, 6)()
-    turn(0)
+    ag_wave(0, 1, NSUB - 1)
     second_rows()
+    ag_hop(0, 2, (), 0, NSUB // 2)
     spread(0)
-    ag_hop(0, 2)
+    ag_hop(0, 2, (), NSUB // 2, NSUB)
     for k in range(1, NZ):
         xr_copy(1, k).start()
     build_own(1, 0)
@@ -474,9 +508,10 @@
     ])
     kept_rows(1)
     share(1)
-    ag_hop(1, 1)
+    ag_wave(1, 1, NSUB - 1)
+    ag_hop(1, 2, (), 0, NSUB // 2)
     spread(1)
-    ag_hop(1, 2)
+    ag_hop(1, 2, (), NSUB // 2, NSUB)
     sp_copy(1).wait_recv()
     ag_hop(1, 3, [lambda: finish(0), lambda: finish(1), lambda: finish(-1)])
     collect(1)
@@ -491,8 +526,8 @@
         out_copies.extend([own, other])
 
     new_weights = [lambda j=j: new_weight(j) for j in range(NZ)]
-    ag_hop(1, 4, new_weights)
-    ag_hop(1, 5, new_weights)
+    ag_hop(1, 4, new_weights[:4])
+    ag_hop(1, 5, new_weights[4:])
     finish(2)
     finish(-2)
     finish(3)
@@ -558,6 +593,7 @@
         dma((STEPS, NZ)), dma((STEPS, NZ)), dma((STEPS,)), dma((STEPS,)),
         dma((STEPS, n_rep)), dma((STEPS, n_rep)), dma((STEPS, NZ + 1)), dma((STEPS, NZ + 1)),
         dma((2 * NZ,)), dma((NZ,)), dma((NZ,)),
+        pltpu.SemaphoreType.REGULAR((6,)),
     ]
     return pl.pallas_call(
         functools.partial(kernel, n_rep),
@@ -571,7 +607,7 @@
         compiler_params=pltpu.CompilerParams(
             collective_id=0, has_side_effects=True, vmem_limit_bytes=40 << 20
         ),
-    )(inputs, targets, weight, momentum, arranged, jnp.asarray(basis_parts()))
+    )(*[pltpu.with_memory_space_constraint(v, pltpu.HBM) for v in (inputs, targets, weight, momentum, arranged, jnp.asarray(basis_parts()))])
 
 
 def solution(mesh):

time: 98.4 us -> 89.3 us (0.908)
  local copies, waits for them, and re-layouts: 11 us -> 3.33 us
  Pallas kernels: 86.4 us -> 85.3 us
    unnamed x14 -> x2, local copies, waits for them, and re-layouts: 11 us -> 3.33 us
    pallas_call x1, Pallas kernels: 86.4 us -> 85.3 us  [local(): pl.pallas_call(functools.partial(kernel, n_rep), out_shape=(jax.ShapeDtyp...]
where the time goes in v3:
time: 89.3 us
  Pallas kernels  85.3 us (96%)
  local copies, waits for them, and re-layouts  3.33 us (4%)
    pallas_call x1, Pallas kernels, local(): pl.pallas_call(functools.partial(kernel, n_rep), out_shape=(jax.ShapeDtyp...  85.3 us
    unnamed x2, local copies, waits for them, and re-layouts  3.33 us

profile of v3, /device:TPU:1, one launch (start us, length us, event | category | flops | bytes accessed | tf_op | source)
XLA Modules:
  0.0 89.3 jit_solution(16535170696186091579)
XLA Ops:
  0.6 85.3 %shard_map.77 = (bf16[512,2048]{1,0:T(8,128)(2,1)S(1)}, f32[1,512,2048]{2,1,0:T(8,128)S(1)}) custom-call(bf16[2,512,512]{2,1,0:T(8,128)(2,1)} %x_ref.1, bf16[2,512,128]{2,1,0:T(8,128)(2,1)} %t_ref.1, bf16[512,2048]{1,0:T(8,128)(2,1)} %w_ref.1, f32[1,512,2048]{2,1,0:T(8,128)} %m_ref.1, s32[2,128,16]{2,1,0:T(8,128)} %bitcast.3, ...), custom_call_target="tpu_custom_call" | custom-call | tf_op jit(solution)/shard_map/pallas_call | solution.py:598
  85.9 1.3 %copy.10 = bf16[512,2048]{1,0:T(8,128)(2,1)} copy(bf16[512,2048]{1,0:T(8,128)(2,1)S(1)} %get-tuple-element.4) | data formatting | bytes 4194304
  87.3 2.0 %copy.11 = f32[1,512,2048]{2,1,0:T(8,128)} copy(f32[1,512,2048]{2,1,0:T(8,128)S(1)} %get-tuple-element.5) | data formatting | bytes 8388608

commit v4 on v3

--- a/solution.py
+++ b/solution.py
@@ -76,6 +76,7 @@
     along_x = [{"rep": (r // side) * side + lax.rem(r + k, side)} for k in (1, side - 1)]
     along_y = [{"rep": lax.rem(r + k * side, n_rep)} for k in (1, side - 1)]
     along_z = [long_to, short_to]
+    two_on = [{"tp": 2 * zz(2) + c}, {"tp": 2 * zz(-2) + c}]
     if n_rep != side * side:
         along_x, along_y = [], []
     barrier = pltpu.get_barrier_semaphore()
@@ -134,8 +135,8 @@
         high = values.astype(BF16)
         low = (values - high.astype(F32)).astype(BF16)
         out = jnp.dot(table, high, preferred_element_type=F32) + jnp.dot(table, low, preferred_element_type=F32)
-        rm_send[s, j, 0] = out[0:8, :BLOCK] + out[8:16, :BLOCK]
-        rm_send[s, j, 1] = out[16:24, BLOCK:] + out[24:32, BLOCK:]
+        rm_send[s, 0, j] = out[0:8, :BLOCK] + out[8:16, :BLOCK]
+        rm_send[s, 1, j] = out[16:24, BLOCK:] + out[24:32, BLOCK:]
 
     def early():
         loads["bt"].wait()
@@ -177,6 +178,9 @@
             if k == 0:
                 ys[s, 0, rows] = acc[:, :BLOCK].astype(BF16)
                 ys[s, 1, rows] = acc[:, BLOCK:].astype(BF16)
+                for u in range(i * NSUB // 2, (i + 1) * NSUB // 2):
+                    for way in range(2):
+                        rs_copy(s, way, 1, u).start()
 
     def rs_copy(s, way, h, u):
         slot = h - 1 if way == 0 else 3 + h
@@ -186,11 +190,6 @@
         else:
             src = rl.at[s, slot - 1, rows]
         return remote(src, rl.at[s, slot, rows], rs_send.at[s, slot, u], rs_recv.at[s, slot, u], (long_to, short_to)[way])
-
-    def rs_first(s):
-        for u in range(NSUB):
-            for way in range(2):
-                rs_copy(s, way, 1, u).start()
 
     def rs_wave(s, h, u):
         rows = pl.ds(u * SUB, SUB)
@@ -298,22 +297,15 @@
             xr_send.at[s, to], xr_land.at[s, z], xr_ssem.at[s, k], xr_rsem.at[s, k], {"tp": 2 * to + c}
         )
 
-    def rm_copy(s, k):
-        to = lax.rem(me + k, 2 * NZ)
-        return remote(
-            rm_send.at[s, to // 2, to % 2], rm_land.at[s, me], rm_ssem.at[s, k], rm_rsem.at[s, k], {"tp": to}
-        )
+    def rm_copy(s):
+        return remote(rm_send.at[s, o], rm_land.at[s], rm_ssem.at[s], rm_rsem.at[s], partner)
 
     def kept_rows(s):
         for k in range(1, NZ):
             xr_copy(s, k).wait_recv()
-        for k in range(1, 2 * NZ):
-            rm_copy(s, k).wait_recv()
         xr_land[s, z] = xr_send[s, z]
-        rm_land[s, me] = rm_send[s, z, c]
         table = xr_land[s].reshape(NZ * 16, TOK)
         out = jnp.dot(table, ef[s, c, z], preferred_element_type=F32) * (1.0 / TOK)
-        out += 0.9 * rm_land[s].reshape(NZ * 16, BLOCK)
         s_send[s] = out.astype(BF16).reshape(NZ, 16, BLOCK)
 
     def sa_copy(s, k):
@@ -338,6 +330,10 @@
     def spread(s):
         for k in range(1, NZ):
             sa_copy(s, k).wait_recv()
+        rm_copy(s).wait_recv()
+        own, other = rm_send[s, c], rm_land[s]
+        rows = jnp.concatenate([jnp.where(c == 0, own, other), jnp.where(c == 0, other, own)], axis=1)
+        sn[s, c] = (sn[s, c].astype(F32) + 0.9 * rows).astype(BF16)
         for k in range(1, n_rep):
             pl_copy(s, k).start()
         sp_copy(s).start()
@@ -403,23 +399,18 @@
 
     ready(0)
     forward(0, 0)
-    rs_first(0)
+    told(0, along_z)
+    tell(1, two_on)
     ready(1)
     forward(0, 1)
     pairs[0].wait_recv()
-    told(0, along_z)
-    tell(1, along_z)
     arrange(0)
     build_rows(0)
-    told(1, along_z)
-    tell(2, along_z)
     ready(2)
     ready(3)
-
-    def send_rows():
-        told(2, along_z)
-        for k in range(1, NZ):
-            xr_copy(0, k).start()
+    told(1, two_on)
+    for k in range(1, NZ):
+        xr_copy(0, k).start()
 
     def pass_on(k, before, after):
         def act():
@@ -427,10 +418,6 @@
             tell(k + 1, after)
 
         return act
-
-    def send_products(s):
-        for k in range(1, 2 * NZ):
-            rm_copy(s, k).start()
 
     def second_rows():
         loads["x1"].wait()
@@ -451,13 +438,14 @@
 
     rs_rest(0, [
         lambda: forward(0, 2),
-        lambda: (products(0)(), send_rows()),
+        products(0),
         lambda: (products(2)(), pass_on(3, along_x, along_y)()),
         lambda: forward(0, 3),
         products(4),
         products(6),
-        lambda: (send_products(0), loads["t"].wait()),
+        lambda: (rm_copy(0).start(), loads["t"].wait()),
         lambda: turn(0),
+        second_rows,
         lambda: (two(build_replicas, 0, 0)(), pass_on(4, along_y, along_y)()),
         two(build_replicas, 0, 2),
         two(build_replicas, 0, 4),
@@ -466,7 +454,6 @@
     kept_rows(0)
     share(0)
     ag_wave(0, 1, NSUB - 1)
-    second_rows()
     ag_hop(0, 2, (), 0, NSUB // 2)
     spread(0)
     ag_hop(0, 2, (), NSUB // 2, NSUB)
@@ -483,14 +470,12 @@
         update(0, order[k][0])
         update(0, order[k][1])
         forward(1, k)
-        if k == 0:
-            rs_first(1)
         if k == 1:
             ag_hop(0, 4)
 
     def last_gain():
         gain(4)
-        send_products(1)
+        rm_copy(1).start()
 
     rs_rest(1, [
         lambda: gain(1),
@@ -514,7 +499,6 @@
     ag_hop(1, 2, (), NSUB // 2, NSUB)
     sp_copy(1).wait_recv()
     ag_hop(1, 3, [lambda: finish(0), lambda: finish(1), lambda: finish(-1)])
-    collect(1)
     out_copies = []
 
     def new_weight(j):
@@ -525,13 +509,11 @@
         other.start()
         out_copies.extend([own, other])
 
-    new_weights = [lambda j=j: new_weight(j) for j in range(NZ)]
-    ag_hop(1, 4, new_weights[:4])
-    ag_hop(1, 5, new_weights[4:])
-    finish(2)
-    finish(-2)
-    finish(3)
-    finish(-3)
+    ag_hop(1, 4, [lambda: finish(2), lambda: finish(-2)])
+    collect(1)
+    for j in range(NZ):
+        new_weight(j)
+    ag_hop(1, 5, [lambda: finish(3), lambda: finish(-3)])
     finish(4)
 
     for copy in out_copies:
@@ -551,8 +533,7 @@
         for k in range(1, NZ):
             xr_copy(s, k).wait_send()
             sa_copy(s, k).wait_send()
-        for k in range(1, 2 * NZ):
-            rm_copy(s, k).wait_send()
+        rm_copy(s).wait_send()
         for k in range(1, n_rep):
             pl_copy(s, k).wait_send()
         sp_copy(s).wait_send()
@@ -582,14 +563,14 @@
         pltpu.VMEM((BLOCK, ROWS), BF16),
         pltpu.VMEM((STEPS, NZ, 16, TOK), BF16),
         pltpu.VMEM((STEPS, NZ, 16, TOK), BF16),
-        pltpu.VMEM((STEPS, NZ, 2, 8, BLOCK), F32),
-        pltpu.VMEM((STEPS, 2 * NZ, 8, BLOCK), F32),
+        pltpu.VMEM((STEPS, 2, NZ, 8, BLOCK), F32),
+        pltpu.VMEM((STEPS, NZ, 8, BLOCK), F32),
         pltpu.VMEM((STEPS, NZ, 16, BLOCK), BF16),
         pltpu.VMEM((STEPS, 2, NZ, 16, BLOCK), BF16),
         pltpu.VMEM((STEPS, n_rep, NZ, 16, BLOCK), BF16),
         dma((24,)), dma((11,)), dma((11,)),
         dma((STEPS, 7, NSUB)), dma((STEPS, 7, NSUB)), dma((STEPS, 7, NSUB)), dma((STEPS, 7, NSUB)),
-        dma((STEPS, NZ)), dma((STEPS, NZ)), dma((STEPS, 2 * NZ)), dma((STEPS, 2 * NZ)),
+        dma((STEPS, NZ)), dma((STEPS, NZ)), dma((STEPS,)), dma((STEPS,)),
         dma((STEPS, NZ)), dma((STEPS, NZ)), dma((STEPS,)), dma((STEPS,)),
         dma((STEPS, n_rep)), dma((STEPS, n_rep)), dma((STEPS, NZ + 1)), dma((STEPS, NZ + 1)),
         dma((2 * NZ,)), dma((NZ,)), dma((NZ,)),

time: 89.3 us -> 85.1 us (0.953)
  Pallas kernels: 85.3 us -> 81.1 us
    pallas_call x1, Pallas kernels: 85.3 us -> 81.1 us  [local(): pl.pallas_call(functools.partial(kernel, n_rep), out_shape=(jax.ShapeDtyp...]
where the time goes in v4:
time: 85.1 us
  Pallas kernels  81.1 us (95%)
  local copies, waits for them, and re-layouts  3.33 us (4%)
    pallas_call x1, Pallas kernels, local(): pl.pallas_call(functools.partial(kernel, n_rep), out_shape=(jax.ShapeDtyp...  81.1 us
    unnamed x2, local copies, waits for them, and re-layouts  3.33 us

profile of v4, /device:TPU:1, one launch (start us, length us, event | category | flops | bytes accessed | tf_op | source)
XLA Modules:
  0.0 85.1 jit_solution(12841992061681259941)
XLA Ops:
  0.6 81.1 %shard_map.77 = (bf16[512,2048]{1,0:T(8,128)(2,1)S(1)}, f32[1,512,2048]{2,1,0:T(8,128)S(1)}) custom-call(bf16[2,512,512]{2,1,0:T(8,128)(2,1)} %x_ref.1, bf16[2,512,128]{2,1,0:T(8,128)(2,1)} %t_ref.1, bf16[512,2048]{1,0:T(8,128)(2,1)} %w_ref.1, f32[1,512,2048]{2,1,0:T(8,128)} %m_ref.1, s32[2,128,16]{2,1,0:T(8,128)} %bitcast.3, ...), custom_call_target="tpu_custom_call" | custom-call | tf_op jit(solution)/shard_map/pallas_call | solution.py:579
  81.7 1.3 %copy.10 = bf16[512,2048]{1,0:T(8,128)(2,1)} copy(bf16[512,2048]{1,0:T(8,128)(2,1)S(1)} %get-tuple-element.4) | data formatting | bytes 4194304
  83.1 2.0 %copy.11 = f32[1,512,2048]{2,1,0:T(8,128)} copy(f32[1,512,2048]{2,1,0:T(8,128)S(1)} %get-tuple-element.5) | data formatting | bytes 8388608

commit v5 on v4

--- a/solution.py
+++ b/solution.py
@@ -41,7 +41,7 @@
     x_ref, t_ref, w_ref, m_ref, idx_ref, bt_ref,
     w_out, m_out,
     xa, xt, tv, wb, mb, iv, bt, frow, left, prow, lu,
-    yp, ys, rl, ef, lx, xr_send, xr_land, rm_send, rm_land, s_send, sn, sall,
+    yp, ys, rl, ef, lx, xr_send, xr_land, rm_send, rm_land, s_send, sn, ps, sall,
     load_sem, pair_send, pair_recv, rs_send, rs_recv, ag_send, ag_recv,
     xr_ssem, xr_rsem, rm_ssem, rm_rsem, sa_ssem, sa_rsem, sp_ssem, sp_rsem,
     pl_ssem, pl_rsem, fw_ssem, fw_rsem, out_sem, outp_ssem, outp_rsem, token,
@@ -317,9 +317,13 @@
     def sp_copy(s):
         return remote(sn.at[s, c], sn.at[s, c], sp_ssem.at[s], sp_rsem.at[s], partner)
 
-    def pl_copy(s, k):
+    parts_of = ((0, 2), (2, 5), (5, 8))
+
+    def pl_copy(s, k, g):
+        low, high = parts_of[g]
         return remote(
-            sn.at[s, c], sall.at[s, r], pl_ssem.at[s, k], pl_rsem.at[s, k], {"rep": lax.rem(r + k, n_rep)}
+            ps.at[s, low:high], sall.at[s, r, low:high], pl_ssem.at[s, k, g], pl_rsem.at[s, k, g],
+            {"rep": lax.rem(r + k, n_rep)},
         )
 
     def share(s):
@@ -327,24 +331,35 @@
             sa_copy(s, k).start()
         sn[s, c, z] = s_send[s, z]
 
-    def spread(s):
-        for k in range(1, NZ):
+    def blend(s, g):
+        for i in range(*parts_of[g]):
+            j = zz(d * steps_out[i])
+            own, other = rm_send[s, c, j], rm_land[s, j]
+            rows = jnp.concatenate([jnp.where(c == 0, own, other), jnp.where(c == 0, other, own)], axis=0)
+            total = (sn[s, c, j].astype(F32) + 0.9 * rows).astype(BF16)
+            sn[s, c, j] = total
+            ps[s, i] = total
+
+    def spread(s, near):
+        for k in (1, NZ - 1) if near else range(2, NZ - 1):
             sa_copy(s, k).wait_recv()
-        rm_copy(s).wait_recv()
-        own, other = rm_send[s, c], rm_land[s]
-        rows = jnp.concatenate([jnp.where(c == 0, own, other), jnp.where(c == 0, other, own)], axis=1)
-        sn[s, c] = (sn[s, c].astype(F32) + 0.9 * rows).astype(BF16)
+        if near:
+            rm_copy(s).wait_recv()
+        for g in (2,) if near else (0, 1):
+            blend(s, g)
+            for k in range(1, n_rep):
+                pl_copy(s, k, g).start()
+        if not near:
+            sp_copy(s).start()
+            sall[s, r] = ps[s]
+
+    def collect(s, g):
         for k in range(1, n_rep):
-            pl_copy(s, k).start()
-        sp_copy(s).start()
-        sall[s, r] = sn[s, c]
-
-    def collect(s):
-        for k in range(1, n_rep):
-            pl_copy(s, k).wait_recv()
-
-    def update(s, j):
-        stack = sall[s, :, j].reshape(lanes, BLOCK)
+            pl_copy(s, k, g).wait_recv()
+
+    def update(s, i):
+        j = zz(d * steps_out[i])
+        stack = sall[s, :, i].reshape(lanes, BLOCK)
         for i in range(4):
             rows = pl.ds(i * 256, 256)
             change = jnp.dot(lu[s, j, rows], stack, preferred_element_type=F32)
@@ -454,8 +469,9 @@
     kept_rows(0)
     share(0)
     ag_wave(0, 1, NSUB - 1)
+    spread(0, True)
     ag_hop(0, 2, (), 0, NSUB // 2)
-    spread(0)
+    spread(0, False)
     ag_hop(0, 2, (), NSUB // 2, NSUB)
     for k in range(1, NZ):
         xr_copy(1, k).start()
@@ -464,11 +480,14 @@
     sp_copy(0).wait_recv()
     gain(0)
     ag_hop(0, 3)
-    collect(0)
+    collect(0, 0)
 
     for k in range(4):
-        update(0, order[k][0])
-        update(0, order[k][1])
+        if k == 1:
+            collect(0, 1)
+            collect(0, 2)
+        update(0, 2 * k)
+        update(0, 2 * k + 1)
         forward(1, k)
         if k == 1:
             ag_hop(0, 4)
@@ -494,25 +513,28 @@
     kept_rows(1)
     share(1)
     ag_wave(1, 1, NSUB - 1)
+    spread(1, True)
     ag_hop(1, 2, (), 0, NSUB // 2)
-    spread(1)
+    spread(1, False)
     ag_hop(1, 2, (), NSUB // 2, NSUB)
     sp_copy(1).wait_recv()
     ag_hop(1, 3, [lambda: finish(0), lambda: finish(1), lambda: finish(-1)])
     out_copies = []
 
-    def new_weight(j):
-        update(1, j)
-        own = pltpu.make_async_copy(wb.at[j, half_own], w_out.at[:, cols(j, c)], out_sem.at[j])
+    def new_weight(i):
+        update(1, i)
+        j = zz(d * steps_out[i])
+        own = pltpu.make_async_copy(wb.at[j, half_own], w_out.at[:, cols(j, c)], out_sem.at[i])
         own.start()
-        other = remote(wb.at[j, half_other], w_out.at[:, cols(j, c)], outp_ssem.at[j], outp_rsem.at[j], partner)
+        other = remote(wb.at[j, half_other], w_out.at[:, cols(j, c)], outp_ssem.at[i], outp_rsem.at[i], partner)
         other.start()
         out_copies.extend([own, other])
 
     ag_hop(1, 4, [lambda: finish(2), lambda: finish(-2)])
-    collect(1)
-    for j in range(NZ):
-        new_weight(j)
+    for g in range(3):
+        collect(1, g)
+    for i in range(NZ):
+        new_weight(i)
     ag_hop(1, 5, [lambda: finish(3), lambda: finish(-3)])
     finish(4)
 
@@ -535,7 +557,8 @@
             sa_copy(s, k).wait_send()
         rm_copy(s).wait_send()
         for k in range(1, n_rep):
-            pl_copy(s, k).wait_send()
+            for g in range(3):
+                pl_copy(s, k, g).wait_send()
         sp_copy(s).wait_send()
 
 
@@ -567,12 +590,13 @@
         pltpu.VMEM((STEPS, NZ, 8, BLOCK), F32),
         pltpu.VMEM((STEPS, NZ, 16, BLOCK), BF16),
         pltpu.VMEM((STEPS, 2, NZ, 16, BLOCK), BF16),
+        pltpu.VMEM((STEPS, NZ, 16, BLOCK), BF16),
         pltpu.VMEM((STEPS, n_rep, NZ, 16, BLOCK), BF16),
         dma((24,)), dma((11,)), dma((11,)),
         dma((STEPS, 7, NSUB)), dma((STEPS, 7, NSUB)), dma((STEPS, 7, NSUB)), dma((STEPS, 7, NSUB)),
         dma((STEPS, NZ)), dma((STEPS, NZ)), dma((STEPS,)), dma((STEPS,)),
         dma((STEPS, NZ)), dma((STEPS, NZ)), dma((STEPS,)), dma((STEPS,)),
-        dma((STEPS, n_rep)), dma((STEPS, n_rep)), dma((STEPS, NZ + 1)), dma((STEPS, NZ + 1)),
+        dma((STEPS, n_rep, 3)), dma((STEPS, n_rep, 3)), dma((STEPS, NZ + 1)), dma((STEPS, NZ + 1)),
         dma((2 * NZ,)), dma((NZ,)), dma((NZ,)),
         pltpu.SemaphoreType.REGULAR((6,)),
     ]

time: 85.1 us -> 85.2 us (level)
  no operation moved by 1% of the time
where the time goes in v5:
time: 85.2 us
  Pallas kernels  81.2 us (95%)
  local copies, waits for them, and re-layouts  3.33 us (4%)
    pallas_call x1, Pallas kernels, local(): pl.pallas_call(functools.partial(kernel, n_rep), out_shape=(jax.ShapeDtyp...  81.2 us
    unnamed x2, local copies, waits for them, and re-layouts  3.33 us

profile of v5, /device:TPU:1, one launch (start us, length us, event | category | flops | bytes accessed | tf_op | source)
XLA Modules:
  0.0 85.2 jit_solution(4800643518424015332)
XLA Ops:
  0.6 81.2 %shard_map.77 = (bf16[512,2048]{1,0:T(8,128)(2,1)S(1)}, f32[1,512,2048]{2,1,0:T(8,128)S(1)}) custom-call(bf16[2,512,512]{2,1,0:T(8,128)(2,1)} %x_ref.1, bf16[2,512,128]{2,1,0:T(8,128)(2,1)} %t_ref.1, bf16[512,2048]{1,0:T(8,128)(2,1)} %w_ref.1, f32[1,512,2048]{2,1,0:T(8,128)} %m_ref.1, s32[2,128,16]{2,1,0:T(8,128)} %bitcast.3, ...), custom_call_target="tpu_custom_call" | custom-call | tf_op jit(solution)/shard_map/pallas_call | solution.py:603
  81.8 1.3 %copy.10 = bf16[512,2048]{1,0:T(8,128)(2,1)} copy(bf16[512,2048]{1,0:T(8,128)(2,1)S(1)} %get-tuple-element.4) | data formatting | bytes 4194304
  83.1 2.0 %copy.11 = f32[1,512,2048]{2,1,0:T(8,128)} copy(f32[1,512,2048]{2,1,0:T(8,128)S(1)} %get-tuple-element.5) | data formatting | bytes 8388608

commit v6 on v4

--- a/solution.py
+++ b/solution.py
@@ -457,29 +457,28 @@
     ag_hop(0, 2, (), 0, NSUB // 2)
     spread(0)
     ag_hop(0, 2, (), NSUB // 2, NSUB)
+    build_own(1, 0)
+    build_own(1, 1)
+    ag_hop(0, 3)
     for k in range(1, NZ):
         xr_copy(1, k).start()
-    build_own(1, 0)
-    build_own(1, 1)
     sp_copy(0).wait_recv()
     gain(0)
-    ag_hop(0, 3)
+    gain(1)
+    gain(-1)
+    ag_hop(0, 4)
     collect(0)
 
     for k in range(4):
         update(0, order[k][0])
         update(0, order[k][1])
         forward(1, k)
-        if k == 1:
-            ag_hop(0, 4)
 
     def last_gain():
         gain(4)
         rm_copy(1).start()
 
     rs_rest(1, [
-        lambda: gain(1),
-        lambda: gain(-1),
         lambda: gain(2),
         lambda: gain(-2),
         lambda: (ag_hop(0, 5), gain(3)),
@@ -537,6 +536,20 @@
         for k in range(1, n_rep):
             pl_copy(s, k).wait_send()
         sp_copy(s).wait_send()
+
+
+def settle(w_ref, m_ref, w_out, m_out, sem):
+    copies = []
+    for k in range(8):
+        rows = pl.ds(k * 64, 64)
+        copies.append(pltpu.make_async_copy(m_ref.at[0, rows], m_out.at[0, rows], sem.at[k]))
+    for k in range(4):
+        rows = pl.ds(k * 128, 128)
+        copies.append(pltpu.make_async_copy(w_ref.at[rows], w_out.at[rows], sem.at[8 + k]))
+    for copy in copies:
+        copy.start()
+    for copy in copies:
+        copy.wait()
 
 
 def local(n_rep, inputs, targets, weight, momentum, indices):
@@ -576,7 +589,7 @@
         dma((2 * NZ,)), dma((NZ,)), dma((NZ,)),
         pltpu.SemaphoreType.REGULAR((6,)),
     ]
-    return pl.pallas_call(
+    new_weight, new_momentum = pl.pallas_call(
         functools.partial(kernel, n_rep),
         out_shape=(
             jax.ShapeDtypeStruct(weight.shape, BF16),
@@ -589,6 +602,17 @@
             collective_id=0, has_side_effects=True, vmem_limit_bytes=40 << 20
         ),
     )(*[pltpu.with_memory_space_constraint(v, pltpu.HBM) for v in (inputs, targets, weight, momentum, arranged, jnp.asarray(basis_parts()))])
+    return pl.pallas_call(
+        settle,
+        out_shape=(
+            jax.ShapeDtypeStruct(weight.shape, BF16),
+            jax.ShapeDtypeStruct(momentum.shape, F32),
+        ),
+        in_specs=[any_space] * 2,
+        out_specs=(pl.BlockSpec(memory_space=pltpu.HBM),) * 2,
+        scratch_shapes=[dma((12,))],
+        compiler_params=pltpu.CompilerParams(vmem_limit_bytes=1 << 20),
+    )(new_weight, new_momentum)
 
 
 def solution(mesh):

time: 85.1 us -> 83.6 us (0.982)
  local copies, waits for them, and re-layouts: 3.33 us -> 0 us
  Pallas kernels: 81.1 us -> 82.7 us
    unnamed x2 -> x0, local copies, waits for them, and re-layouts: 3.33 us -> none
    pallas_call x0 -> x1, Pallas kernels: none -> 2.75 us  [local(): pl.pallas_call(settle, out_shape=(jax.ShapeDtypeStruct(weight.shape, BF16...]
    pallas_call x1, Pallas kernels: 81.1 us -> 80 us  [local(): pl.pallas_call(functools.partial(kernel, n_rep), out_shape=(jax.ShapeDtyp...]
where the time goes in v6:
time: 83.6 us; the launch traced here: 83.5 us
  Pallas kernels  82.7 us (99%)
    pallas_call x1, Pallas kernels, local(): pl.pallas_call(functools.partial(kernel, n_rep), out_shape=(jax.ShapeDtyp...  80 us
    pallas_call x1, Pallas kernels, local(): pl.pallas_call(settle, out_shape=(jax.ShapeDtypeStruct(weight.shape, BF16...  2.75 us

profile of v6, /device:TPU:1, one launch (start us, length us, event | category | flops | bytes accessed | tf_op | source)
XLA Modules:
  0.0 83.5 jit_solution(12994138178332232950)
XLA Ops:
  0.6 80.0 %shard_map.77 = (bf16[512,2048]{1,0:T(8,128)(2,1)S(1)}, f32[1,512,2048]{2,1,0:T(8,128)S(1)}) custom-call(bf16[2,512,512]{2,1,0:T(8,128)(2,1)} %x_ref.1, bf16[2,512,128]{2,1,0:T(8,128)(2,1)} %t_ref.1, bf16[512,2048]{1,0:T(8,128)(2,1)} %w_ref.1, f32[1,512,2048]{2,1,0:T(8,128)} %m_ref.1, s32[2,128,16]{2,1,0:T(8,128)} %bitcast.3, ...), custom_call_target="tpu_custom_call" | custom-call | tf_op jit(solution)/shard_map/pallas_call | solution.py:592
  80.6 2.8 %shard_map.78 = (bf16[512,2048]{1,0:T(8,128)(2,1)}, f32[1,512,2048]{2,1,0:T(8,128)}) custom-call(bf16[512,2048]{1,0:T(8,128)(2,1)S(1)} %get-tuple-element.4.w_ref, f32[1,512,2048]{2,1,0:T(8,128)S(1)} %get-tuple-element.5.m_ref), custom_call_target="tpu_custom_call" | custom-call | tf_op jit(solution)/shard_map/pallas_call | solution.py:605
